TPU v7x, 512 devices: a whole 4x8x8 slice. The times are simulated.
512 devices in a mesh: tm: 64 (over y, z_hi, core), height: 8 (over x, z_lo).
Axes of the slice: x: 4, y: 8, z: 8 (z_hi: 4, z_lo: 2; z = z_hi * 2 + z_lo), core: 2. Of those that a mesh axis runs over, the one named last changes fastest.
Arguments:
- coarse_input: bfloat16 [192, 32, 16, 512], P('tm', 'height'), may hold values from -450 to 450
- cotangent: bfloat16 [192, 64, 32, 256], P('tm', 'height'), may hold values from -45 to 45
- conv_kernel: bfloat16 [27, 512, 256], P(None, None, 'tm'), may hold values from -0.0546875 to 0.0546875
- short_kernel: bfloat16 [1, 512, 256], P(None, None, 'tm'), may hold values from -0.25 to 0.25
- norm_gain: float32 [512], replicated, may hold values from 0.5 to 2
- norm_bias: float32 [512], replicated, may hold values from -3 to 3
- frame_lengths: int32 [64], replicated, may hold values from 1 to 3, 97 in all
- row_lengths: int32 [8], replicated, may hold values from 1 to 4, 17 in all
Outputs:
- coarse_grad: float32 [192, 32, 16, 512], P('tm', 'height')
Inputs may be any that keep to these rules, and one draw needn't show every extreme that they name: `frame_lengths`: the entries sum to 97, and some tm index holds 3 frames. `row_lengths`: the entries sum to 17, and some height index holds 4 coarse rows.
All inputs are finite; a program needn't handle non-finite values.
Results may differ from a plain program's by a relative error of at most 0.00035.
Values may be sent and summed in bfloat16 or wider, within the bound.
A program may use at most 128 MiB of HBM per device.

v0:
```python
import jax
import jax.numpy as jnp
from jax import lax
from jax.sharding import PartitionSpec as P

GROUPS = 32


EPSILON = 1e-06


def extended_2(array, sides, width):
    for axis, dim in sides:
        size, length = (lax.axis_size(axis), array.shape[dim])
        up = [(i, (i + 1) % size) for i in range(size - 1)]
        down = [(j, i) for i, j in up]
        last = lax.slice_in_dim(array, length - width, length, axis=dim)
        first = lax.slice_in_dim(array, 0, width, axis=dim)
        before = lax.ppermute(last, axis, up)
        after = lax.ppermute(first, axis, down)
        array = jnp.concatenate([before, array, after], axis=dim)
    return array


def from_behind(value, axis, steps):
    count = lax.axis_size(axis)
    first, last = (max(0, -steps), min(count, count - steps))
    return lax.ppermute(value, axis, [(source, source + steps) for source in range(first, last)])


def group_totals(values, groups):
    shaped = values.reshape(values.shape[:-1] + (groups, values.shape[-1] // groups))
    return jnp.sum(shaped, axis=(0, 1, 2, 4))


def per_channel(statistics, channels):
    return jnp.repeat(statistics, channels // statistics.shape[0])


def contribution(padded, weights, frames, fine_rows, fine_cols):
    running = None
    for time_tap in range(3):
        windows = [
            padded[
                2 - time_tap : 2 - time_tap + frames,
                2 - row_tap : 2 - row_tap + fine_rows,
                2 - col_tap : 2 - col_tap + fine_cols,
            ]
            for row_tap in range(3)
            for col_tap in range(3)
        ]
        stacked = jnp.stack(windows, axis=3)
        tap_term = lax.dot_general(
            stacked,
            weights[9 * time_tap : 9 * time_tap + 9],
            (((3, 4), (0, 2)), ((), ())),
            preferred_element_type=jnp.float32,
        )
        running = tap_term if running is None else running + tap_term
    center = padded[0:frames, 1 : 1 + fine_rows, 1 : 1 + fine_cols]
    skip_term = lax.dot_general(
        center, weights[27], (((3,), (1,)), ((), ())), preferred_element_type=jnp.float32
    )
    return jnp.stack([running, skip_term])


def shards(
    coarse_input,
    cotangent,
    conv_kernel,
    short_kernel,
    norm_gain,
    norm_bias,
    frame_lengths,
    row_lengths,
):
    frames, coarse_rows, coarse_cols, width_mid = coarse_input.shape
    fine_rows = cotangent.shape[1]
    fine_cols = cotangent.shape[2]
    time_index = lax.axis_index("tm")
    stripe_index = lax.axis_index("height")
    live_frames = frame_lengths[time_index]
    live_rows = row_lengths[stripe_index]
    frame_ok = jnp.arange(frames) < live_frames
    row_ok = jnp.arange(coarse_rows) < live_rows
    valid_slot = (frame_ok[:, None] & row_ok[None, :])[:, :, None, None]
    values = coarse_input.astype(jnp.float32)
    masked = jnp.where(valid_slot, values, 0.0)
    group_sums, squares = lax.psum(
        (group_totals(masked, GROUPS), group_totals(masked * masked, GROUPS)), ("tm", "height")
    )
    total_count = (jnp.sum(frame_lengths) * jnp.sum(row_lengths)).astype(jnp.float32) * float(
        coarse_cols * (width_mid // GROUPS)
    )
    group_mean = group_sums / total_count
    inverse_std = lax.rsqrt(squares / total_count - group_mean * group_mean + EPSILON)
    inverse_chan = per_channel(inverse_std, width_mid)
    normed = (values - per_channel(group_mean, width_mid)) * inverse_chan
    pre_act = normed * norm_gain + norm_bias
    sigmoid_pre = jax.nn.sigmoid(pre_act)
    silu_slope = sigmoid_pre * (1.0 + pre_act * (1.0 - sigmoid_pre))
    fine_live = 2 * live_rows
    fine_index = jnp.arange(fine_rows)
    rows_kept = jnp.where(
        (fine_index < fine_live)[None, :, None, None], cotangent, jnp.zeros((), cotangent.dtype)
    )
    last_row = lax.dynamic_index_in_dim(rows_kept, fine_live - 1, axis=1, keepdims=False)
    row_pair = jnp.stack([rows_kept[:, 0], last_row], axis=1)
    row_edges = extended_2(row_pair, (("height", 1),), 1)
    row_above = row_edges[:, 0]
    row_below = row_edges[:, 3]
    inner_rows = jnp.where(
        (fine_index == fine_live)[None, :, None, None], row_below[:, None], rows_kept
    )
    row_tail = jnp.where(fine_live == fine_rows, row_below, jnp.zeros_like(row_below))
    extended = jnp.concatenate([row_above[:, None], inner_rows, row_tail[:, None]], axis=1)
    following = from_behind(extended[0], "tm", -1)
    second_own = jnp.where(live_frames >= 2, extended[1], following)
    second_after = from_behind(second_own, "tm", -1)
    frames_ahead = jnp.stack([following, second_after])
    stream = jnp.concatenate([extended, frames_ahead], axis=0)
    position = jnp.arange(frames + 2)
    source = jnp.minimum(
        jnp.where(position < live_frames, position, frames + position - live_frames), frames + 1
    )
    keep_frame = position < live_frames + 2
    ordered = jnp.where(
        keep_frame[:, None, None, None],
        jnp.take(stream, source, axis=0),
        jnp.zeros((), stream.dtype),
    )
    padded = jnp.pad(ordered, ((0, 0), (0, 0), (1, 1), (0, 0)))
    kernels = jnp.concatenate([conv_kernel, short_kernel], axis=0)
    full_kernels = lax.all_gather(kernels, "tm", axis=2, tiled=True)
    gradients = contribution(padded, full_kernels, frames, fine_rows, fine_cols)
    pooled = gradients.reshape(2, frames, coarse_rows, 2, coarse_cols, 2, width_mid).sum(
        axis=(3, 5)
    )
    grad_hat = pooled[0] * silu_slope * norm_gain
    slope_sum, slope_cross = lax.psum(
        (
            group_totals(jnp.where(valid_slot, grad_hat, 0.0), GROUPS),
            group_totals(jnp.where(valid_slot, grad_hat * normed, 0.0), GROUPS),
        ),
        ("tm", "height"),
    )
    result = (
        inverse_chan
        * (
            grad_hat
            - (per_channel(slope_sum, width_mid) + normed * per_channel(slope_cross, width_mid))
            / total_count
        )
        + pooled[1]
    )
    return jnp.where(valid_slot, result, 0.0)


def solution(mesh):
    return jax.shard_map(
        shards,
        mesh=mesh,
        in_specs=(
            P("tm", "height", None, None),
            P("tm", "height", None, None),
            P(None, None, "tm"),
            P(None, None, "tm"),
            P(),
            P(),
            P(),
            P(),
        ),
        out_specs=P("tm", "height", None, None),
        check_vma=False,
    )
```

profile of v0, /device:TPU:1, one launch (start us, length us, event | category | flops | bytes accessed | tf_op | source)
XLA Modules:
  0.0 322.0 jit_solution(3905681060376524035)
XLA Ops:
  8.2 1.3 dynamic_slice.11
  11.3 1.3 collective-permute-start.1
  12.6 5.5 %collective-permute-start = (bf16[3,1,32,256]{3,2,1,0:T(8,128)(2,1)S(1)}, bf16[3,1,32,256]{3,2,1,0:T(8,128)(2,1)S(1)}, u32[]{:S(2)}, u32[]{:S(2)}) collective-permute-start(bf16[3,1,32,256]{3,2,1,0:T(8,128)(2,1)S(1)} %get-tuple-element.23), channel_id=1, source_target_pairs={{0,1},{1,2},{2,3},{3,4},{4,5},{5,6},{6,7},{8,9},{9,10},{10,11},{11... | collective-permute-start | bytes 147464 | tf_op jit(solution)/shard_map/ppermute | solution.py:19
  18.0 1.2 dynamic_slice.10
  22.0 109.6 %all-reduce.2 = (f32[32]{0:T(128)S(1)}, f32[32]{0:T(128)S(1)}) all-reduce(f32[32]{0:T(128)S(1)} %reduce_sum.98, f32[32]{0:T(128)S(1)} %reduce_sum.75), channel_id=1, replica_groups=mesh['tm'=64,'height'=8] {'tm','height'}, use_global_device_ids=true, to_apply=%region_7.8 | all-reduce | flops 64 | bytes 512 | tf_op jit(solution)/shard_map/psum | solution.py:89
  131.7 1.3 reduce_sum.76
  133.0 1.3 reduce_sum.80
  136.7 3.3 %collective-permute-start.2 = (bf16[10,32,256]{2,1,0:T(8,128)(2,1)S(1)}, bf16[10,32,256]{2,1,0:T(8,128)(2,1)S(1)}, u32[]{:S(2)}, u32[]{:S(2)}) collective-permute-start(bf16[10,32,256]{2,1,0:T(8,128)(2,1)S(1)} %maximum_bitcast_fusion), channel_id=1, source_target_pairs={{8,0},{16,8},{24,16},{32,24},{40,32},{48,40},{56,48},{64,56},{72,6... | collective-permute-start | bytes 491528 | tf_op jit(solution)/shard_map/ppermute | solution.py:28
  141.7 4.4 %collective-permute-done.2 = bf16[10,32,256]{2,1,0:T(8,128)(2,1)S(1)} collective-permute-done((bf16[10,32,256]{2,1,0:T(8,128)(2,1)S(1)}, bf16[10,32,256]{2,1,0:T(8,128)(2,1)S(1)}, u32[]{:S(2)}, u32[]{:S(2)}) %collective-permute-start.2) | collective-permute-done | bytes 163872 | tf_op jit(solution)/shard_map/ppermute | solution.py:28
  146.1 1.9 collective-permute-start.3
  149.0 4.7 %collective-permute-done.3 = bf16[10,32,256]{2,1,0:T(8,128)(2,1)S(1)} collective-permute-done((bf16[10,32,256]{2,1,0:T(8,128)(2,1)S(1)}, bf16[10,32,256]{2,1,0:T(8,128)(2,1)S(1)}, u32[]{:S(2)}, u32[]{:S(2)}) %collective-permute-start.3) | collective-permute-done | bytes 163872 | tf_op jit(solution)/shard_map/ppermute | solution.py:28
  157.7 1.2 fusion.88
  158.8 1.4 fusion.48
  165.7 2.1 slice.169
  167.8 1.3 copy.64
  169.1 9.6 %fusion.98 = (bf16[9,512,256]{1,0,2:T(8,128)(2,1)}, bf16[9,512,256]{1,0,2:T(8,128)(2,1)}, bf16[9,512,256]{1,0,2:T(8,128)(2,1)}) fusion(bf16[28,512,256]{1,0,2:T(8,128)(2,1)} %all-gather.2.cloned.1.call-done), kind=kLoop, calls=%fused_computation.148 | loop fusion | bytes 14155776 | tf_op jit(solution)/shard_map/slice | solution.py:55
  178.7 7.2 %copy.63 = bf16[9,512,256]{2,1,0:T(8,128)(2,1)} copy(bf16[9,512,256]{1,0,2:T(8,128)(2,1)} %get-tuple-element.17) | data formatting | bytes 4718592
  185.8 5.9 %copy.62 = bf16[9,512,256]{2,1,0:T(8,128)(2,1)S(1)} copy(bf16[9,512,256]{1,0,2:T(8,128)(2,1)} %get-tuple-element.18) | data formatting | bytes 4718592
  191.8 7.1 %copy.61 = bf16[9,512,256]{2,1,0:T(8,128)(2,1)} copy(bf16[9,512,256]{1,0,2:T(8,128)(2,1)} %get-tuple-element.16) | data formatting | bytes 4718592
  198.9 4.9 %fusion.16 = f32[3,8,32,512]{3,2,0,1:T(8,128)S(1)} fusion(bf16[9,512,256]{2,1,0:T(8,128)(2,1)} %copy.63, bf16[3,8,32,9,256]{4,2,1,0,3:T(8,128)(2,1)} %copy-done.4), kind=kOutput, calls=%fused_computation.14 | convolution fusion | flops 1811939328 | bytes 7471104 | tf_op jit(solution)/shard_map/dot_general | solution.py:53
  203.8 2.0 fusion.11
  205.8 4.0 %fusion.8 = f32[3,8,32,512]{3,2,1,0:T(8,128)S(1)} fusion(f32[3,8,32,512]{3,2,0,1:T(8,128)S(1)} %fusion.16, f32[3,8,32,512]{3,2,0,1:T(8,128)S(1)} %fusion.11, bf16[3,8,32,9,256]{4,2,3,1,0:T(8,128)(2,1)} %fusion.56, bf16[9,512,256]{2,1,0:T(8,128)(2,1)S(1)} %copy-done), kind=kOutput, calls=%fused_computation.11 | convolution fusion | flops 1812725760 | bytes 10616832 | tf_op jit(solution)/shard_map/dot_general | solution.py:53
  211.1 1.4 convolution_bitcast_fusion
  213.6 100.4 %all-reduce.1 = (f32[32]{0:T(128)S(1)}, f32[32]{0:T(128)S(1)}) all-reduce(f32[32]{0:T(128)S(1)} %reduce_sum.105, f32[32]{0:T(128)S(1)} %reduce_sum.102), channel_id=1, replica_groups=mesh['tm'=64,'height'=8] {'tm','height'}, use_global_device_ids=true, to_apply=%region_14.15 | all-reduce | flops 64 | bytes 512 | tf_op jit(solution)/shard_map/psum | solution.py:140
  (86 shorter events, 20.9 us)
Async XLA Ops:
  6.5 159.1 %all-gather.2.cloned.1.call-start = ((), (), s32[]{:S(2)}) async-start(), calls=%async_computation | async-start | bytes 8519680 | tf_op jit(solution)/shard_map/all_gather | solution.py:134
  11.3 124.2 %collective-permute-start.1 = (bf16[3,1,32,256]{3,2,1,0:T(8,128)(2,1)S(1)}, bf16[3,1,32,256]{3,2,1,0:T(8,128)(2,1)S(1)}, u32[]{:S(2)}, u32[]{:S(2)}) collective-permute-start(bf16[3,1,32,256]{3,2,1,0:T(8,128)(2,1)S(1)} %get-tuple-element.24), channel_id=1, source_target_pairs={{1,0},{2,1},{3,2},{4,3},{5,4},{6,5},{7,6},{9,8},{10,9},{11,10},{12... | collective-permute-start | bytes 147464 | tf_op jit(solution)/shard_map/ppermute | solution.py:20
  12.6 124.1 %collective-permute-start = (bf16[3,1,32,256]{3,2,1,0:T(8,128)(2,1)S(1)}, bf16[3,1,32,256]{3,2,1,0:T(8,128)(2,1)S(1)}, u32[]{:S(2)}, u32[]{:S(2)}) collective-permute-start(bf16[3,1,32,256]{3,2,1,0:T(8,128)(2,1)S(1)} %get-tuple-element.23), channel_id=1, source_target_pairs={{0,1},{1,2},{2,3},{3,4},{4,5},{5,6},{6,7},{8,9},{9,10},{10,11},{11... | collective-permute-start | bytes 147464 | tf_op jit(solution)/shard_map/ppermute | solution.py:19
  136.7 9.5 %collective-permute-start.2 = (bf16[10,32,256]{2,1,0:T(8,128)(2,1)S(1)}, bf16[10,32,256]{2,1,0:T(8,128)(2,1)S(1)}, u32[]{:S(2)}, u32[]{:S(2)}) collective-permute-start(bf16[10,32,256]{2,1,0:T(8,128)(2,1)S(1)} %maximum_bitcast_fusion), channel_id=1, source_target_pairs={{8,0},{16,8},{24,16},{32,24},{40,32},{48,40},{56,48},{64,56},{72,6... | collective-permute-start | bytes 491528 | tf_op jit(solution)/shard_map/ppermute | solution.py:28
  146.1 7.5 %collective-permute-start.3 = (bf16[10,32,256]{2,1,0:T(8,128)(2,1)S(1)}, bf16[10,32,256]{2,1,0:T(8,128)(2,1)S(1)}, u32[]{:S(2)}, u32[]{:S(2)}) collective-permute-start(bf16[10,32,256]{2,1,0:T(8,128)(2,1)S(1)} %fusion.93), channel_id=1, source_target_pairs={{8,0},{16,8},{24,16},{32,24},{40,32},{48,40},{56,48},{64,56},{72,6... | collective-permute-start | bytes 491528 | tf_op jit(solution)/shard_map/ppermute | solution.py:28
  157.1 4.1 %copy-start.2 = (bf16[3,8,32,9,256]{4,2,1,0,3:T(8,128)(2,1)}, bf16[3,8,32,9,256]{4,2,1,0,3:T(8,128)(2,1)S(1)}, u32[]{:S(2)}) copy-start(bf16[3,8,32,9,256]{4,2,1,0,3:T(8,128)(2,1)S(1)} %get-tuple-element.19) | copy-start | bytes 10616836
  157.7 7.1 %copy-start.4 = (bf16[3,8,32,9,256]{4,2,1,0,3:T(8,128)(2,1)}, bf16[3,8,32,9,256]{4,2,1,0,3:T(8,128)(2,1)S(1)}, u32[]{:S(2)}) copy-start(bf16[3,8,32,9,256]{4,2,1,0,3:T(8,128)(2,1)S(1)} %fusion.80) | copy-start | bytes 10616836
  198.9 4.9 %copy-start.3 = (bf16[3,8,32,9,256]{4,2,1,0,3:T(8,128)(2,1)S(1)}, bf16[3,8,32,9,256]{4,2,1,0,3:T(8,128)(2,1)}, u32[]{:S(2)}) copy-start(bf16[3,8,32,9,256]{4,2,1,0,3:T(8,128)(2,1)} %copy-done.2) | copy-start | bytes 10616836
  203.8 2.0 copy-start
  211.1 1.8 copy-start.1
  211.1 1.8 copy-start.5
  211.1 1.8 copy-start.6
Sparse Core Ops, SparseCore 0:
  10.7 110.2 all-gather.1
where the time goes:
time: 323 us; the launch traced here: 322 us
  blocking collectives  210 us (65%)
  local copies, waits for them, and re-layouts  50 us (15%)
  between operations  16.8 us (5%)
  matrix products  12.3 us (4%)
  starting transfers between devices  12 us (4%)
  other arithmetic  11.7 us (4%)
  waiting for transfers between devices  9.14 us (3%)
    psum x1, blocking collectives, shards(): lax.psum((group_totals(masked, GROUPS), group_totals(masked * masked, GRO...  110 us
    psum x1, blocking collectives, shards(): lax.psum((group_totals(jnp.where(valid_slot, grad_hat, 0.0), GROUPS), gro...  100 us
    unnamed x40, local copies, waits for them, and re-layouts  31 us
    dot_general x3, matrix products, contribution(): lax.dot_general(stacked, weights[9 * time_tap:9 * time_tap + 9], (((3, 4)...  10.9 us
    slice x1, local copies, waits for them, and re-layouts, contribution(): weights[9 * time_tap:9 * time_tap + 9]  9.56 us
    ppermute x2, waiting for transfers between devices, from_behind(): lax.ppermute(value, axis, [(source, source + steps) for source in range(f...  9.12 us
  transfers between devices with their start and end apart: 5, of which 2 were waited for; matrix products, arithmetic and copies ran while one was open for 7% of the time, Pallas kernels for 0%

commit v1 on v0

v1 whole, which is shorter than its diff:
```python
import functools

import jax
import jax.numpy as jnp
from jax import lax
from jax.experimental import pallas as pl
from jax.experimental.pallas import tpu as pltpu
from jax.sharding import PartitionSpec as P

EPSILON = 1e-06
COUNT = 422144.0
TAPS = ((0, 16), (16, 12))
BF = jnp.bfloat16
F32 = jnp.float32


def mod(value, n):
    return lax.rem(value + n, n)


class Table:
    def __init__(self, send, recv):
        self.send, self.recv, self.entries, self.count = send, recv, {}, 0

    def add(self, name, src, dst, device):
        self.entries[name] = (src, dst, device, self.count)
        self.count += 1

    def get(self, name):
        src, dst, device, at = self.entries[name]
        return pltpu.make_async_remote_copy(
            src_ref=src() if callable(src) else src,
            dst_ref=dst() if callable(dst) else dst,
            send_sem=self.send.at[at],
            recv_sem=self.recv.at[at],
            device_id=device,
            device_id_type=pl.DeviceIdType.MESH,
        )

    def start(self, *names):
        for name in names:
            self.get(name).start()

    def arrive(self, *names):
        for name in names:
            self.get(name).wait_recv()

    def sent(self, *names):
        for name in names:
            self.get(name).wait_send()


def kernel(
    fl_ref, rl_ref, y_ref, g_ref, wc_ref, ws_ref, gain_ref, bias_ref, out_ref,
    whole, mine, slots, rows32, ahead, edge_out, edge_in, padded, windows,
    acc, skip, hat, slope, ar, ar_send, ar_recv, small_send, small_recv,
    send0, recv0, send1, recv1,
):
    tm, height = lax.axis_index("tm"), lax.axis_index("height")
    y, h, c = tm // 8, lax.rem(tm // 2, 4), lax.rem(tm, 2)
    x, zl = height // 2, lax.rem(height, 2)
    fl, rl = fl_ref[tm], rl_ref[height]
    fl_next = fl_ref[mod(tm + 1, 64)]

    def at(y_=y, h_=h, c_=c, x_=x, z_=zl):
        return (y_ * 8 + h_ * 2 + c_, x_ * 2 + z_)

    partners = []
    for d in range(1, 8):
        q = lax.rem(h * 2 + c + d, 8)
        partners.append(at(h_=q // 2, c_=lax.rem(q, 2)))
        partners.append(at(y_=lax.rem(y + d, 8)))
    for d in range(1, 4):
        partners.append(at(x_=lax.rem(x + d, 4)))
        partners.append(at(x_=lax.rem(x + d, 4), c_=1 - c))
    for d in range(4):
        partners.append(at(h_=lax.rem(h + d, 4), z_=1 - zl))
    for d in (1, 2, 62, 63):
        partners.append((lax.rem(tm + d, 64), height))
    for d in (1, 7):
        partners.append((tm, lax.rem(height + d, 8)))
    barrier = pltpu.get_barrier_semaphore()
    for partner in partners:
        pl.semaphore_signal(barrier, inc=1, device_id=partner, device_id_type=pl.DeviceIdType.MESH)

    def ar_copy(turn, step, d):
        if step == 0:
            own = x * 2 + c
            other = lax.rem(own + d, 8)
            device = at(x_=other // 2, c_=lax.rem(other, 2))
        elif step == 1:
            own = y
            device = at(y_=lax.rem(own + d, 8))
        else:
            own = h * 2 + zl
            other = lax.rem(own + d, 8)
            device = at(h_=other // 2, z_=lax.rem(other, 2))
        place = ar.at[turn, step, own]
        return own, pltpu.make_async_remote_copy(
            src_ref=place, dst_ref=place,
            send_sem=ar_send.at[turn, step, d - 1], recv_sem=ar_recv.at[turn, step, d - 1],
            device_id=device, device_id_type=pl.DeviceIdType.MESH,
        )

    def ar_begin(turn, step, value):
        own, _ = ar_copy(turn, step, 1)
        ar[turn, step, own] = value
        for d in range(1, 8):
            ar_copy(turn, step, d)[1].start()

    def ar_end(turn, step):
        for d in range(1, 8):
            ar_copy(turn, step, d)[1].wait_recv()
        return jnp.sum(ar[turn, step], axis=0)

    def tile_of(first, second):
        parts = [v[:, 128 * k : 128 * k + 128] for v in (first, second) for k in range(4)]
        return jnp.concatenate(parts, axis=0)

    def row_of(tile, base):
        return jnp.concatenate([tile[base + k : base + k + 1] for k in range(4)], axis=1)

    same = (lax.broadcasted_iota(jnp.int32, (128, 128), 0) >> 4) == (
        lax.broadcasted_iota(jnp.int32, (128, 128), 1) >> 4
    )
    group_ones = jnp.where(same, 1.0, 0.0).astype(F32)

    def group_total(tile):
        return jnp.dot(tile, group_ones, precision=lax.Precision.HIGHEST, preferred_element_type=F32)

    first = jnp.zeros((16, 512), F32)
    second = jnp.zeros((16, 512), F32)
    for f in range(3):
        for r in range(4):
            live = jnp.where((f < fl) & (r < rl), 1.0, 0.0).astype(F32)
            value = y_ref[f, r].astype(F32) * live
            first = first + value
            second = second + value * value
    stats = tile_of(jnp.sum(first, axis=0, keepdims=True), jnp.sum(second, axis=0, keepdims=True))
    mine[0:27] = wc_ref[...]
    mine[27:28] = ws_ref[...]

    def table(role):
        t0, taps = TAPS[role]
        half = taps // 2
        t = Table(send0 if role == 0 else send1, recv0 if role == 0 else recv1)

        def piece(column, block, lo=0, n=taps):
            row = pl.multiple_of(block * 32, 32)
            return whole.at[pl.ds(t0 + lo, n), column, pl.ds(row, 32)]

        for d in range(1, 4):
            device = at(h_=lax.rem(h + d, 4), c_=role)
            lane = pl.multiple_of(x * 128, 128)
            src = mine.at[pl.ds(t0, taps), :, pl.ds(lane, 128)]
            t.add(f"a{d}0", src, slots.at[pl.ds(0, taps), h * 2 + 0], device)
            t.add(f"a{d}1", src, slots.at[pl.ds(0, taps), h * 2 + 1], device)
        t.add("as", src, slots.at[pl.ds(0, taps), h * 2 + 1 - role], at(c_=role))
        columns = [x, mod(x - 1, 4), mod(x + 1, 4), mod(x + 2, 4)]
        blocks = [y]
        for s in range(1, 4):
            blocks += [mod(y - s, 8), mod(y + s, 8)]
        blocks.append(mod(y + 4, 8))
        left, right = at(x_=mod(x - 1, 4)), at(x_=mod(x + 1, 4))
        up, down = at(y_=mod(y + 1, 8)), at(y_=mod(y - 1, 8))
        for k in range(8 if role == 0 else 1):
            b = blocks[k]
            for name, column, lo, n, device in (
                (f"xr{k}", 0, 0, taps, right),
                (f"xl{k}", 0, 0, taps, left),
                (f"or{k}", 1, 0, half, right),
                (f"ol{k}", 2, half, taps - half, left),
            ):
                ref = piece(columns[column], b, lo, n)
                t.add(name, ref, ref, device)
        for j in range(1 if role == 0 else 4):
            for s in range(4):
                ref = piece(columns[j], mod(y - s, 8), 0, half if s == 3 else taps)
                t.add(f"yp{j}{s}", ref, ref, up)
                ref = piece(columns[j], mod(y + s, 8), half if s == 3 else 0, taps - half if s == 3 else taps)
                t.add(f"ym{j}{s}", ref, ref, down)
        for k in range(8):
            for j in range(4):
                ref = piece(columns[j], blocks[k])
                t.add(f"d{k}{j}", ref, ref, at(c_=1 - role))
        return t

    tables = (table(0), table(1))

    def stage_a_send():
        for role in (0, 1):
            @pl.when(c == 0)
            def _():
                for d in range(1, 4):
                    tables[role].start(f"a{d}0")

            @pl.when(c == 1)
            def _():
                for d in range(1, 4):
                    tables[role].start(f"a{d}1")

            @pl.when(c == 1 - role)
            def _():
                tables[role].start("as")

    def stage_a_sent():
        for role in (0, 1):
            @pl.when(c == 0)
            def _():
                for d in range(1, 4):
                    tables[role].sent(f"a{d}0")

            @pl.when(c == 1)
            def _():
                for d in range(1, 4):
                    tables[role].sent(f"a{d}1")

            @pl.when(c == 1 - role)
            def _():
                tables[role].sent("as")

    def stage_a_arrive(role):
        t0, taps = TAPS[role]
        t = tables[role]
        lane = pl.multiple_of(x * 128, 128)
        slots[0:taps, h * 2 + role] = mine[t0 : t0 + taps, :, pl.ds(lane, 128)]
        for d in range(1, 4):
            t.arrive(f"a{d}0", f"a{d}1")
        t.arrive("as")
        for s in range(8):
            rows32[0:taps, 4 * s : 4 * s + 4] = slots[0:taps, s].astype(F32)
        row = pl.multiple_of(y * 32, 32)
        whole[t0 : t0 + taps, x, pl.ds(row, 32)] = rows32[0:taps].astype(BF)

    def x_in0(k):
        t = tables[0]
        t.arrive(f"xr{k}")
        t.start(f"or{k}", f"d{k}1")
        t.arrive(f"xl{k}")
        t.start(f"ol{k}", f"d{k}2")

    def o_in0(k):
        t = tables[0]
        t.arrive(f"or{k}", f"ol{k}")
        t.start(f"d{k}3")

    def y_in0(s):
        t = tables[0]
        if s < 4:
            k = 2 * s - 1
            t.arrive(f"yp0{s - 1}")
            t.start(f"yp0{s}", f"xr{k}", f"xl{k}", f"d{k}0")
            t.arrive(f"ym0{s - 1}")
            t.start(f"ym0{s}", f"xr{k + 1}", f"xl{k + 1}", f"d{k + 1}0")
        else:
            t.arrive("yp03", "ym03")
            t.start("xr7", "xl7", "d70")

    def x_in1():
        t = tables[1]
        t.arrive("xr0")
        t.start("or0", "yp10", "ym10", "d01")
        t.arrive("xl0")
        t.start("ol0", "yp20", "ym20", "d02")
        t.arrive("or0", "ol0")
        t.start("yp30", "ym30", "d03")

    def y_in1(s):
        t = tables[1]
        for j in range(4):
            if s < 4:
                t.arrive(f"yp{j}{s - 1}")
                t.start(f"yp{j}{s}", f"d{2 * s - 1}{j}")
                t.arrive(f"ym{j}{s - 1}")
                t.start(f"ym{j}{s}", f"d{2 * s}{j}")
            else:
                t.arrive(f"yp{j}3", f"ym{j}3")
                t.start(f"d7{j}")

    def small_copy(which):
        if which == 0:
            src, dst, device = g_ref.at[pl.ds(0, 2)], ahead.at[pl.ds(0, 2)], (mod(tm - 1, 64), height)
        elif which == 1:
            src, dst, device = g_ref.at[0], ahead.at[2], (lax.rem(tm + 62, 64), height)
        elif which == 2:
            src, dst, device = edge_out.at[1], edge_in.at[0], (tm, mod(height + 1, 8))
        else:
            src, dst, device = edge_out.at[0], edge_in.at[1], (tm, mod(height - 1, 8))
        return pltpu.make_async_remote_copy(
            src_ref=src, dst_ref=dst, send_sem=small_send.at[which], recv_sem=small_recv.at[which],
            device_id=device, device_id_type=pl.DeviceIdType.MESH,
        )

    zero_frame = jnp.zeros((8, 32, 256), BF)
    zero_row = jnp.zeros((32, 256), BF)

    def order_frames():
        small_copy(0).wait_recv()
        small_copy(1).wait_recv()
        has_one = tm < 63
        has_two = jnp.logical_and(has_one, jnp.logical_or(fl_next >= 2, tm < 62))
        following = lax.select(has_one, ahead[0], zero_frame)
        after = lax.select(fl_next >= 2, ahead[1], ahead[2])
        after = lax.select(has_two, after, zero_frame)
        own = [g_ref[0], g_ref[1], g_ref[2]]
        ordered = [
            own[0],
            lax.select(fl >= 2, own[1], following),
            lax.select(fl >= 3, own[2], lax.select(fl == 2, following, after)),
            lax.select(fl >= 3, following, lax.select(fl == 2, after, zero_frame)),
            lax.select(fl >= 3, after, zero_frame),
        ]
        for p in range(5):
            last = ordered[p][1]
            for r in range(8):
                row = ordered[p][r]
                if r >= 2:
                    row = lax.select(r < 2 * rl, row, zero_row)
                if r >= 3 and r % 2 == 1:
                    last = lax.select(r == 2 * rl - 1, row, last)
                padded[p, r + 1] = row
            edge_out[0, p] = ordered[p][0]
            edge_out[1, p] = last
        small_copy(2).start()
        small_copy(3).start()

    def finish_rows():
        small_copy(2).wait_recv()
        small_copy(3).wait_recv()
        for p in range(5):
            above = lax.select(height > 0, edge_in[0, p], zero_row)
            below = lax.select(height < 7, edge_in[1, p], zero_row)
            padded[p, 0] = above
            for r in (2, 4, 6):
                padded[p, r + 1] = lax.select(r == 2 * rl, below, padded[p, r + 1])
            padded[p, 9] = lax.select(rl == 4, below, zero_row)

    def make_windows():
        out_row = lax.broadcasted_iota(jnp.int32, (64, 320), 0)
        in_row = lax.broadcasted_iota(jnp.int32, (64, 320), 1)
        down_by = (in_row >> 5) - 2 * (out_row >> 4)
        along_by = (in_row & 31) - 2 * (out_row & 15)
        choose = []
        for kh in range(3):
            for kw in range(3):
                dr, dc = down_by - (2 - kh), along_by - (1 - kw)
                hit = ((dr == 0) | (dr == 1)) & ((dc == 0) | (dc == 1))
                choose.append(jnp.where(hit, 1.0, 0.0).astype(F32))
        chosen = jnp.concatenate(choose, axis=0).astype(BF)

        def one(f, carry):
            total = jnp.dot(chosen, padded[f].reshape(320, 256), preferred_element_type=F32)
            top = total.astype(BF)
            rest = (total - top.astype(F32)).astype(BF)
            windows[f, 0] = top.reshape(9, 64, 256)
            windows[f, 1] = rest.reshape(9, 64, 256)
            return carry

        lax.fori_loop(0, 5, one, 0)

    def make_slope(total):
        gs = group_total(total) * (1.0 / COUNT)
        mean, msq = gs[0:4], gs[4:8]
        rstd = lax.rsqrt(msq - mean * mean + EPSILON)
        mean_row, rstd_row = row_of(mean, 0), row_of(rstd, 0)
        gain, bias = gain_ref[...], bias_ref[...]

        def one(i, carry):
            value = (y_ref[i // 4, lax.rem(i, 4)].astype(F32) - mean_row) * rstd_row
            pre = value * gain + bias
            sig = jax.nn.sigmoid(pre)
            hat[i] = value
            slope[i] = sig * (1.0 + pre * (1.0 - sig)) * gain
            return carry

        lax.fori_loop(0, 12, one, 0)
        return rstd_row

    pl.semaphore_wait(barrier, len(partners))
    stage_a_send()
    ar_begin(0, 0, stats)
    small_copy(0).start()
    small_copy(1).start()

    @pl.when(c == 0)
    def _():
        stage_a_arrive(0)
        tables[0].start("yp00", "ym00", "xr0", "xl0", "d00")

    @pl.when(c == 1)
    def _():
        stage_a_arrive(1)
        tables[1].start("xr0", "xl0", "yp00", "ym00", "d00")

    ar_begin(0, 1, ar_end(0, 0))

    @pl.when(c == 0)
    def _():
        y_in0(1)
        x_in0(0)

    @pl.when(c == 1)
    def _():
        x_in1()

    ar_begin(0, 2, ar_end(0, 1))
    order_frames()

    @pl.when(c == 0)
    def _():
        y_in0(2)
        x_in0(1)
        o_in0(0)
        x_in0(2)

    @pl.when(c == 1)
    def _():
        y_in1(1)

    finish_rows()
    make_windows()

    @pl.when(c == 0)
    def _():
        y_in0(3)
        o_in0(1)
        x_in0(3)
        o_in0(2)
        x_in0(4)

    @pl.when(c == 1)
    def _():
        y_in1(2)

    rstd_row = make_slope(ar_end(0, 2))

    @pl.when(c == 0)
    def _():
        y_in0(4)
        o_in0(3)
        x_in0(5)
        o_in0(4)
        x_in0(6)
        o_in0(5)
        x_in0(7)
        o_in0(6)
        o_in0(7)
        for k in range(8):
            tables[1].arrive(*[f"d{k}{j}" for j in range(4)])

    @pl.when(c == 1)
    def _():
        y_in1(3)
        y_in1(4)
        for k in range(8):
            tables[0].arrive(*[f"d{k}{j}" for j in range(4)])

    def kernel_rows(first_tap, n):
        block = whole[pl.ds(first_tap, n)]
        return jnp.concatenate([block[:, k].reshape(n * 256, 128) for k in range(4)], axis=1)

    skip[...] = jnp.dot(
        windows[0:3, :, 4].reshape(384, 256), kernel_rows(27, 1), preferred_element_type=F32
    ).reshape(3, 2, 64, 512)
    acc[...] = jnp.zeros_like(acc)

    def taps_of(i, carry):
        kt, kh = i // 3, lax.rem(i, 3)
        lhs = jnp.concatenate(
            [windows[pl.ds(2 - kt, 3), :, kh * 3 + kw].reshape(384, 256) for kw in range(3)], axis=1
        )
        acc[...] += jnp.dot(lhs, kernel_rows(3 * i, 3), preferred_element_type=F32).reshape(3, 2, 64, 512)
        return carry

    lax.fori_loop(0, 9, taps_of, 0)

    one_sum = jnp.zeros((16, 512), F32)
    two_sum = jnp.zeros((16, 512), F32)
    for f in range(3):
        for r in range(4):
            here = slice(16 * r, 16 * r + 16)
            live = jnp.where((f < fl) & (r < rl), 1.0, 0.0).astype(F32)
            grad = (acc[f, 0, here] + acc[f, 1, here]) * slope[4 * f + r]
            slope[4 * f + r] = grad
            one_sum = one_sum + grad * live
            two_sum = two_sum + grad * hat[4 * f + r] * live
    sums = tile_of(jnp.sum(one_sum, axis=0, keepdims=True), jnp.sum(two_sum, axis=0, keepdims=True))
    ar_begin(1, 0, sums)
    ar_begin(1, 1, ar_end(1, 0))
    ar_begin(1, 2, ar_end(1, 1))
    both = group_total(ar_end(1, 2)) * (1.0 / COUNT)
    b_one, b_two = row_of(both, 0), row_of(both, 4)
    for f in range(3):
        for r in range(4):
            here = slice(16 * r, 16 * r + 16)
            live = jnp.where((f < fl) & (r < rl), 1.0, 0.0).astype(F32)
            value = rstd_row * (slope[4 * f + r] - (b_one + hat[4 * f + r] * b_two))
            out_ref[f, r] = (value + (skip[f, 0, here] + skip[f, 1, here])) * live

    stage_a_sent()
    for which in range(4):
        small_copy(which).wait_send()
    for turn in range(2):
        for step in range(3):
            for d in range(1, 8):
                ar_copy(turn, step, d)[1].wait_send()
    for role in (0, 1):
        @pl.when(c == role)
        def _():
            tables[role].sent(*[n for n in tables[role].entries if n[0] != "a"])


def shards(coarse_input, cotangent, conv_kernel, short_kernel, norm_gain, norm_bias, frame_lengths, row_lengths):
    vmem = pl.BlockSpec(memory_space=pltpu.VMEM)
    smem = pl.BlockSpec(memory_space=pltpu.SMEM)
    copies = (7 + 32 + 8 + 32, 7 + 4 + 32 + 32)
    return pl.pallas_call(
        kernel,
        out_shape=jax.ShapeDtypeStruct((3, 4, 16, 512), F32),
        in_specs=[smem, smem] + [vmem] * 6,
        out_specs=vmem,
        scratch_shapes=[
            pltpu.VMEM((28, 4, 256, 128), BF),
            pltpu.VMEM((28, 4, 512), BF),
            pltpu.VMEM((16, 8, 4, 128), BF),
            pltpu.VMEM((16, 32, 128), F32),
            pltpu.VMEM((3, 8, 32, 256), BF),
            pltpu.VMEM((2, 5, 32, 256), BF),
            pltpu.VMEM((2, 5, 32, 256), BF),
            pltpu.VMEM((5, 10, 32, 256), BF),
            pltpu.VMEM((5, 2, 9, 64, 256), BF),
            pltpu.VMEM((3, 2, 64, 512), F32),
            pltpu.VMEM((3, 2, 64, 512), F32),
            pltpu.VMEM((12, 16, 512), F32),
            pltpu.VMEM((12, 16, 512), F32),
            pltpu.VMEM((2, 3, 8, 8, 128), F32),
            pltpu.SemaphoreType.DMA((2, 3, 7)),
            pltpu.SemaphoreType.DMA((2, 3, 7)),
            pltpu.SemaphoreType.DMA((4,)),
            pltpu.SemaphoreType.DMA((4,)),
            pltpu.SemaphoreType.DMA((copies[0],)),
            pltpu.SemaphoreType.DMA((copies[0],)),
            pltpu.SemaphoreType.DMA((copies[1],)),
            pltpu.SemaphoreType.DMA((copies[1],)),
        ],
        compiler_params=pltpu.CompilerParams(
            collective_id=0, has_side_effects=True, vmem_limit_bytes=40 * 1024 * 1024
        ),
    )(
        frame_lengths, row_lengths, coarse_input, cotangent,
        conv_kernel.transpose(0, 2, 1), short_kernel.transpose(0, 2, 1),
        norm_gain.reshape(1, 512), norm_bias.reshape(1, 512),
    )


def solution(mesh):
    return jax.shard_map(
        shards,
        mesh=mesh,
        in_specs=(
            P("tm", "height", None, None),
            P("tm", "height", None, None),
            P(None, None, "tm"),
            P(None, None, "tm"),
            P(),
            P(),
            P(),
            P(),
        ),
        out_specs=P("tm", "height", None, None),
        check_vma=False,
    )
```

time: 323 us -> 87 us (0.27)
  blocking collectives: 210 us -> 0 us
  Pallas kernels: 0 us -> 81.7 us
  local copies, waits for them, and re-layouts: 50 us -> 4.94 us
  between operations: 16.8 us -> 0.03 us
  matrix products: 12.3 us -> 0 us
  starting transfers between devices: 12 us -> 0 us
  other arithmetic: 11.7 us -> 0 us
  waiting for transfers between devices: 9.14 us -> 0 us
    psum x2 -> x0, blocking collectives: 210 us -> none  [the longest x1 110 us: shards(): lax.psum((group_totals(masked, GROUPS), group_totals(masked * masked, GRO...]
    pallas_call x0 -> x1, Pallas kernels: none -> 81.7 us  [shards(): pl.pallas_call(kernel, out_shape=jax.ShapeDtypeStruct((3, 4, 16, 512), F3...]
    unnamed x40 -> x17, local copies, waits for them, and re-layouts: 31 us -> 4.94 us
    dot_general x4 -> x0, matrix products: 12.3 us -> none  [the longest x3 10.9 us: contribution(): lax.dot_general(stacked, weights[9 * time_tap:9 * time_tap + 9], (((3, 4)...]
    ppermute x4 -> x0, starting transfers between devices: 12 us -> none  [the longest x1 5.46 us: extended_2(): before = lax.ppermute(last, axis, up)]
    slice x3 -> x0, local copies, waits for them, and re-layouts: 11.7 us -> none  [the longest x1 9.56 us: contribution(): weights[9 * time_tap:9 * time_tap + 9]]
    ppermute x4 -> x0, waiting for transfers between devices: 9.12 us -> none  [the longest x2 9.12 us: from_behind(): lax.ppermute(value, axis, [(source, source + steps) for source in range(f...]
    reduce_sum x9 -> x0, other arithmetic: 4.81 us -> none  [the longest x6 1.84 us: group_totals(): return jnp.sum(shaped, axis=(0, 1, 2, 4))]
  transfers between devices with their start and end apart: 5 -> 0, of which waited for: 2 -> 0; matrix products, arithmetic and copies ran while one was open for 7% -> 0% of each run, Pallas kernels for 0% -> 0%
where the time goes in v1:
time: 87 us; the launch traced here: 86.6 us
  Pallas kernels  81.7 us (94%)
  local copies, waits for them, and re-layouts  4.94 us (6%)
    pallas_call x1, Pallas kernels, shards(): pl.pallas_call(kernel, out_shape=jax.ShapeDtypeStruct((3, 4, 16, 512), F3...  81.7 us
    unnamed x17, local copies, waits for them, and re-layouts  4.94 us

profile of v1, /device:TPU:1, one launch (start us, length us, event | category | flops | bytes accessed | tf_op | source)
XLA Modules:
  0.0 86.6 jit_solution(7223385171178139340)
XLA Ops:
  0.0 0.0 copy-start.3
  0.0 0.0 copy-start.4
  0.0 0.0 copy-start.6
  0.0 0.0 copy-start.7
  0.0 0.7 copy-done.3
  0.7 0.0 copy-done.4
  0.7 0.0 copy-done.6
  0.7 0.0 copy-done.7
  0.7 0.0 copy-start
  0.7 1.0 %copy-done = bf16[3,8,32,256]{3,2,1,0:T(8,128)(2,1)S(1)} copy-done((bf16[3,8,32,256]{3,2,1,0:T(8,128)(2,1)S(1)}, bf16[3,8,32,256]{3,2,1,0:T(8,128)(2,1)}, u32[]{:S(2)}) %copy-start) | copy-done | bytes 393240
  1.7 0.0 copy-start.1
  1.7 0.9 %copy-done.1 = bf16[3,4,16,512]{3,2,1,0:T(8,128)(2,1)S(1)} copy-done((bf16[3,4,16,512]{3,2,1,0:T(8,128)(2,1)S(1)}, bf16[3,4,16,512]{3,2,1,0:T(8,128)(2,1)}, u32[]{:S(2)}) %copy-start.1) | copy-done | bytes 196632
  2.6 0.0 copy-start.2
  2.6 0.9 %copy-done.2 = bf16[27,512,4]{1,2,0:T(4,128)(2,1)S(1)} copy-done((bf16[27,512,4]{1,2,0:T(4,128)(2,1)S(1)}, bf16[27,512,4]{1,2,0:T(4,128)(2,1)}, u32[]{:S(2)}) %copy-start.2) | copy-done | bytes 110616
  3.5 0.0 copy-start.5
  3.5 0.7 copy-done.5
  4.2 81.7 %shard_map.82 = f32[3,4,16,512]{3,2,1,0:T(8,128)S(1)} custom-call(s32[64]{0:T(128)S(1)} %copy-done.6, s32[8]{0:T(128)S(1)} %copy-done.7, bf16[3,4,16,512]{3,2,1,0:T(8,128)(2,1)S(1)} %copy-done.1, bf16[3,8,32,256]{3,2,1,0:T(8,128)(2,1)S(1)} %copy-done, bf16[27,4,512]{2,1,0:T(4,128)(2,1)S(1)} %bitcast.4, bf16[1,4,512]{2,1,0:T(4,128)(2,1)S(1)} %bitcast.5, ...), custom_call_target="tpu_custom_call" | custom-call | tf_op jit(solution)/shard_map/pallas_call | solution.py:517
  85.9 0.7 copy.10
Async XLA Ops:
  0.0 0.7 copy-start.3
  0.0 0.7 copy-start.4
  0.0 0.7 copy-start.6
  0.0 0.7 copy-start.7
  0.7 1.0 %copy-start = (bf16[3,8,32,256]{3,2,1,0:T(8,128)(2,1)S(1)}, bf16[3,8,32,256]{3,2,1,0:T(8,128)(2,1)}, u32[]{:S(2)}) copy-start(bf16[3,8,32,256]{3,2,1,0:T(8,128)(2,1)} %g_ref.1) | copy-start | bytes 1179652
  1.7 0.9 %copy-start.1 = (bf16[3,4,16,512]{3,2,1,0:T(8,128)(2,1)S(1)}, bf16[3,4,16,512]{3,2,1,0:T(8,128)(2,1)}, u32[]{:S(2)}) copy-start(bf16[3,4,16,512]{3,2,1,0:T(8,128)(2,1)} %y_ref.1) | copy-start | bytes 589828
  2.6 0.9 %copy-start.2 = (bf16[27,512,4]{1,2,0:T(4,128)(2,1)S(1)}, bf16[27,512,4]{1,2,0:T(4,128)(2,1)}, u32[]{:S(2)}) copy-start(bf16[27,512,4]{1,2,0:T(4,128)(2,1)} %param.10) | copy-start | bytes 331780
  3.5 0.7 copy-start.5

commit v2 on v1

v2 whole, which is shorter than its diff:
```python
import functools

import jax
import jax.numpy as jnp
from jax import lax
from jax.experimental import pallas as pl
from jax.experimental.pallas import tpu as pltpu
from jax.sharding import PartitionSpec as P

EPSILON = 1e-06
COUNT = 422144.0
TAPS = ((0, 18), (18, 10))
BF = jnp.bfloat16
F32 = jnp.float32


def mod(value, n):
    return lax.rem(value + n, n)


class Table:
    def __init__(self, send, recv):
        self.send, self.recv, self.entries, self.count = send, recv, {}, 0

    def add(self, name, src, dst, device):
        self.entries[name] = (src, dst, device, self.count)
        self.count += 1

    def get(self, name):
        src, dst, device, at = self.entries[name]
        return pltpu.make_async_remote_copy(
            src_ref=src() if callable(src) else src,
            dst_ref=dst() if callable(dst) else dst,
            send_sem=self.send.at[at],
            recv_sem=self.recv.at[at],
            device_id=device,
            device_id_type=pl.DeviceIdType.MESH,
        )

    def start(self, *names):
        for name in names:
            self.get(name).start()

    def arrive(self, *names):
        for name in names:
            self.get(name).wait_recv()

    def sent(self, *names):
        for name in names:
            self.get(name).wait_send()


def ring_distance(d, n):
    return min(d, n - d)


PLANE = sorted(
    [(dx, dy) for dx in range(4) for dy in range(8) if dx + dy],
    key=lambda d: -(ring_distance(d[0], 4) + ring_distance(d[1], 8)),
)
COLUMN = sorted(
    [(dz, dc) for dz in range(8) for dc in range(2) if dz + dc],
    key=lambda d: -(ring_distance(d[0], 8) + d[1]),
)


def kernel(
    fl_any, rl_any, y_any, g_any, wc_any, ws_any, gain_any, bias_any, out_ref,
    fl_ref, rl_ref, y_ref, g_ref, gain_ref, bias_ref, load_sem,
    whole, mine, slots, rows32, ahead, chosen_next, edge_out, edge_in, padded, windows,
    acc, skip, hat, slope, plane, column, plane_send, plane_recv, column_send, column_recv,
    small_send, small_recv, send0, recv0, send1, recv1,
):
    tm, height = lax.axis_index("tm"), lax.axis_index("height")
    y, h, c = tm // 8, lax.rem(tm // 2, 4), lax.rem(tm, 2)
    x, zl = height // 2, lax.rem(height, 2)
    z = h * 2 + zl

    def at(y_=y, z_=z, c_=c, x_=x):
        return (y_ * 8 + (z_ // 2) * 2 + c_, x_ * 2 + lax.rem(z_, 2))

    def plane_device(d):
        return at(x_=lax.rem(x + d[0], 4), y_=lax.rem(y + d[1], 8))

    def column_device(d):
        return at(z_=lax.rem(z + d[0], 8), c_=lax.rem(c + d[1], 2))

    partners = [plane_device(d) for d in PLANE] + [column_device(d) for d in COLUMN]
    for d in (1, 2, 62, 63):
        partners.append((lax.rem(tm + d, 64), height))
    for d in (1, 7):
        partners.append((tm, lax.rem(height + d, 8)))
    barrier = pltpu.get_barrier_semaphore()
    for partner in partners:
        pl.semaphore_signal(barrier, inc=1, device_id=partner, device_id_type=pl.DeviceIdType.MESH)
    loads = [
        pltpu.make_async_copy(src, dst, load_sem.at[k])
        for k, (src, dst) in enumerate((
            (fl_any, fl_ref), (rl_any, rl_ref), (y_any, y_ref), (wc_any, mine.at[pl.ds(0, 27)]),
            (ws_any, mine.at[pl.ds(27, 1)]), (g_any, g_ref), (gain_any, gain_ref), (bias_any, bias_ref),
        ))
    ]
    for load in loads:
        load.start()
    loads[0].wait()
    loads[1].wait()
    fl, rl = fl_ref[tm], rl_ref[height]
    fl_next = fl_ref[mod(tm + 1, 64)]

    def ar_copy(turn, step, k):
        if step == 0:
            place, device = plane.at[turn, x * 8 + y], plane_device(PLANE[k])
            sems = plane_send.at[turn, k], plane_recv.at[turn, k]
        else:
            place, device = column.at[turn, z * 2 + c], column_device(COLUMN[k])
            sems = column_send.at[turn, k], column_recv.at[turn, k]
        return pltpu.make_async_remote_copy(
            src_ref=place, dst_ref=place, send_sem=sems[0], recv_sem=sems[1],
            device_id=device, device_id_type=pl.DeviceIdType.MESH,
        )

    def ar_begin(turn, step, value):
        if step == 0:
            plane[turn, x * 8 + y] = value
        else:
            column[turn, z * 2 + c] = value
        for k in range((31, 15)[step]):
            ar_copy(turn, step, k).start()

    def ar_end(turn, step):
        for k in range((31, 15)[step]):
            ar_copy(turn, step, k).wait_recv()
        return jnp.sum((plane, column)[step][turn], axis=0)

    def row_of(tile, base):
        return jnp.concatenate([tile[base + k : base + k + 1] for k in range(4)], axis=1)

    lane_i = lax.broadcasted_iota(jnp.int32, (128, 128), 0)
    lane_j = lax.broadcasted_iota(jnp.int32, (128, 128), 1)
    fold = jnp.where((lane_i >> 4) == (lane_j & 7), 1.0, 0.0).astype(F32)
    unfold = jnp.where((lane_i & 7) == (lane_j >> 4), 1.0, 0.0).astype(F32)
    own_lanes = lax.broadcasted_iota(jnp.int32, (8, 128), 0) == (
        lax.broadcasted_iota(jnp.int32, (8, 128), 1) >> 3
    )

    def fold_groups(first, second):
        parts = [v[:, 128 * k : 128 * k + 128] for v in (first, second) for k in range(4)]
        tile = jnp.concatenate(parts, axis=0)
        sums = jnp.dot(tile, fold, precision=lax.Precision.HIGHEST, preferred_element_type=F32)
        return jnp.sum(jnp.where(own_lanes, sums, 0.0), axis=0, keepdims=True)

    def unfold_groups(row):
        tile = jnp.where(own_lanes, jnp.broadcast_to(row, (8, 128)), 0.0)
        return jnp.dot(tile, unfold, precision=lax.Precision.HIGHEST, preferred_element_type=F32)

    loads[2].wait()
    first = jnp.zeros((16, 512), F32)
    second = jnp.zeros((16, 512), F32)
    for f in range(3):
        for r in range(4):
            live = jnp.where((f < fl) & (r < rl), 1.0, 0.0).astype(F32)
            value = y_ref[f, r].astype(F32) * live
            first = first + value
            second = second + value * value
    stats = fold_groups(jnp.sum(first, axis=0, keepdims=True), jnp.sum(second, axis=0, keepdims=True))
    for load in loads[3:]:
        load.wait()

    def table(role):
        t0, taps = TAPS[role]
        half = taps // 2
        t = Table(send0 if role == 0 else send1, recv0 if role == 0 else recv1)

        def piece(column, block, lo=0, n=taps):
            row = pl.multiple_of(block * 32, 32)
            return whole.at[pl.ds(t0 + lo, n), column, pl.ds(row, 32)]

        lane = pl.multiple_of(x * 128, 128)
        src = mine.at[pl.ds(t0, taps), :, pl.ds(lane, 128)]
        place = slots.at[pl.ds(0, taps), h * 2 + c]
        for d in range(1, 4):
            device = at(z_=mod(z + (2 * zl - 1) * d, 8), c_=role)
            t.add(f"a{d}0", src, place, device)
            t.add(f"a{d}1", src, place, device)
        t.add("as", src, place, at(c_=role))
        columns = [x, mod(x - 1, 4), mod(x + 1, 4), mod(x + 2, 4)]
        blocks = [y]
        for s in range(1, 4):
            blocks += [mod(y - s, 8), mod(y + s, 8)]
        blocks.append(mod(y + 4, 8))
        left, right = at(x_=mod(x - 1, 4)), at(x_=mod(x + 1, 4))
        up, down = at(y_=mod(y + 1, 8)), at(y_=mod(y - 1, 8))
        parts = ((0, half), (half, taps - half))
        for k in range(8 if role == 0 else 1):
            for q in (0, 1):
                ref = piece(columns[0], blocks[k], *parts[q])
                t.add(f"xr{k}{q}", ref, ref, right)
                t.add(f"xl{k}{q}", ref, ref, left)
            ref = piece(columns[1], blocks[k], *parts[0])
            t.add(f"or{k}", ref, ref, right)
            ref = piece(columns[2], blocks[k], *parts[1])
            t.add(f"ol{k}", ref, ref, left)
        for j in range(1 if role == 0 else 4):
            for s in range(4):
                for q in (0, 1):
                    if s < 3 or q == 0:
                        ref = piece(columns[j], mod(y - s, 8), *parts[q])
                        t.add(f"yp{j}{s}{q}", ref, ref, up)
                    if s < 3 or q == 1:
                        ref = piece(columns[j], mod(y + s, 8), *parts[q])
                        t.add(f"ym{j}{s}{q}", ref, ref, down)
        for k in range(8):
            for j in range(4):
                ref = piece(columns[j], blocks[k])
                t.add(f"d{k}{j}", ref, ref, at(c_=1 - role))
        return t

    tables = (table(0), table(1))

    def stage_a_send():
        for role in (0, 1):
            @pl.when(c == 0)
            def _():
                for d in range(1, 4):
                    tables[role].start(f"a{d}0")

            @pl.when(c == 1)
            def _():
                for d in range(1, 4):
                    tables[role].start(f"a{d}1")

            @pl.when(c == 1 - role)
            def _():
                tables[role].start("as")

    def stage_a_sent():
        for role in (0, 1):
            @pl.when(c == 0)
            def _():
                for d in range(1, 4):
                    tables[role].sent(f"a{d}0")

            @pl.when(c == 1)
            def _():
                for d in range(1, 4):
                    tables[role].sent(f"a{d}1")

            @pl.when(c == 1 - role)
            def _():
                tables[role].sent("as")

    def stage_a_arrive(role):
        t0, taps = TAPS[role]
        t = tables[role]
        lane = pl.multiple_of(x * 128, 128)
        slots[0:taps, h * 2 + role] = mine[t0 : t0 + taps, :, pl.ds(lane, 128)]
        for d in range(1, 4):
            t.arrive(f"a{d}0", f"a{d}1")
        t.arrive("as")
        row = pl.multiple_of(y * 32, 32)
        for s in range(8):
            rows32[0:taps, 4 * s : 4 * s + 4] = slots[0:taps, s].astype(F32)
        whole[t0 : t0 + taps, x, pl.ds(row, 32)] = rows32[0:taps].astype(BF)

    def begin(role):
        t = tables[role]
        for q in (0, 1):
            both = [f"yp00{q}", f"ym00{q}", f"xr0{q}", f"xl0{q}"]
            t.start(*(both if role == 0 else both[2:] + both[:2]))
        t.start("d00")

    def x_in0(k):
        t = tables[0]
        t.arrive(f"xr{k}0")
        t.start(f"or{k}")
        t.arrive(f"xl{k}1")
        t.start(f"ol{k}")
        t.arrive(f"xr{k}1")
        t.start(f"d{k}1")
        t.arrive(f"xl{k}0")
        t.start(f"d{k}2")

    def o_in0(k):
        t = tables[0]
        t.arrive(f"or{k}", f"ol{k}")
        t.start(f"d{k}3")

    def y_in0(s):
        t = tables[0]
        k = 2 * s - 1
        for q in (0, 1):
            if s < 4 or q == 0:
                t.arrive(f"yp0{s - 1}{q}")
                if s < 3 or (s == 3 and q == 0):
                    t.start(f"yp0{s}{q}")
                t.start(f"xr{k}{q}", f"xl{k}{q}")
            if s < 4 or q == 1:
                t.arrive(f"ym0{s - 1}{q}")
                if s < 3 or (s == 3 and q == 1):
                    t.start(f"ym0{s}{q}")
                m = min(k + 1, 7)
                t.start(f"xr{m}{q}", f"xl{m}{q}")
        t.start(f"d{k}0")
        if s < 4:
            t.start(f"d{k + 1}0")

    def x_in1():
        t = tables[1]
        for q in (0, 1):
            t.arrive(f"xr0{q}")
            t.start(f"yp10{q}", f"ym10{q}")
            if q == 0:
                t.start("or0")
        for q in (1, 0):
            t.arrive(f"xl0{q}")
            if q == 1:
                t.start("ol0")
            t.start(f"yp20{q}", f"ym20{q}")
        t.start("d01", "d02")

    def o_in1():
        t = tables[1]
        t.arrive("or0")
        t.start("yp300", "ym300")
        t.arrive("ol0")
        t.start("yp301", "ym301", "d03")

    def y_in1(s, chains=(0, 1, 2, 3)):
        t = tables[1]
        for j in chains:
            for q in (0, 1):
                if s < 4 or q == 0:
                    t.arrive(f"yp{j}{s - 1}{q}")
                    if s < 3 or (s == 3 and q == 0):
                        t.start(f"yp{j}{s}{q}")
                if s < 4 or q == 1:
                    t.arrive(f"ym{j}{s - 1}{q}")
                    if s < 3 or (s == 3 and q == 1):
                        t.start(f"ym{j}{s}{q}")
            t.start(f"d{2 * s - 1}{j}")
            if s < 4:
                t.start(f"d{2 * s}{j}")

    def small_copy(which):
        before, sibling = (mod(tm - 1, 64), height), at(c_=1 - c)
        if which == 0:
            src, dst, device = g_ref.at[pl.ds(0, 2)], ahead.at[pl.ds(0, 2)], sibling
        elif which == 1:
            src, dst, device = g_ref.at[0], ahead.at[0], before
        elif which == 2:
            src, dst, device = chosen_next, ahead.at[1], before
        elif which == 3:
            src, dst, device = ahead.at[0], ahead.at[2], sibling
        elif which == 4:
            src, dst, device = edge_out.at[1], edge_in.at[0], (tm, mod(height + 1, 8))
        else:
            src, dst, device = edge_out.at[0], edge_in.at[1], (tm, mod(height - 1, 8))
        return pltpu.make_async_remote_copy(
            src_ref=src, dst_ref=dst, send_sem=small_send.at[which], recv_sem=small_recv.at[which],
            device_id=device, device_id_type=pl.DeviceIdType.MESH,
        )

    zero_frame = jnp.zeros((8, 32, 256), BF)
    zero_row = jnp.zeros((32, 256), BF)

    def frames_begin():
        @pl.when(c == 0)
        def _():
            small_copy(1).start()

        @pl.when(c == 1)
        def _():
            small_copy(0).start()

    def frames_choose():
        @pl.when(c == 0)
        def _():
            small_copy(0).wait_recv()
            chosen_next[...] = lax.select(fl >= 2, g_ref[1], ahead[0])
            small_copy(2).start()

    def frames_pass():
        @pl.when(c == 1)
        def _():
            small_copy(1).wait_recv()
            small_copy(3).start()

    def order_frames():
        @pl.when(c == 0)
        def _():
            small_copy(3).wait_recv()

        @pl.when(c == 1)
        def _():
            small_copy(2).wait_recv()

        has_one = tm < 63
        has_two = jnp.logical_and(has_one, jnp.logical_or(fl_next >= 2, tm < 62))
        following = lax.select(has_one, ahead[0], zero_frame)
        after = lax.select(jnp.logical_or(c == 1, fl_next >= 2), ahead[1], ahead[2])
        after = lax.select(has_two, after, zero_frame)
        own = [g_ref[0], g_ref[1], g_ref[2]]
        ordered = [
            own[0],
            lax.select(fl >= 2, own[1], following),
            lax.select(fl >= 3, own[2], lax.select(fl == 2, following, after)),
            lax.select(fl >= 3, following, lax.select(fl == 2, after, zero_frame)),
            lax.select(fl >= 3, after, zero_frame),
        ]
        for p in range(5):
            last = ordered[p][1]
            for r in range(8):
                row = ordered[p][r]
                if r >= 2:
                    row = lax.select(r < 2 * rl, row, zero_row)
                if r >= 3 and r % 2 == 1:
                    last = lax.select(r == 2 * rl - 1, row, last)
                padded[p, r + 1] = row
            edge_out[0, p] = ordered[p][0]
            edge_out[1, p] = last
        small_copy(4).start()
        small_copy(5).start()

    def finish_rows():
        small_copy(4).wait_recv()
        small_copy(5).wait_recv()
        for p in range(5):
            above = lax.select(height > 0, edge_in[0, p], zero_row)
            below = lax.select(height < 7, edge_in[1, p], zero_row)
            padded[p, 0] = above
            for r in (2, 4, 6):
                padded[p, r + 1] = lax.select(r == 2 * rl, below, padded[p, r + 1])
            padded[p, 9] = lax.select(rl == 4, below, zero_row)

    def make_windows():
        out_row = lax.broadcasted_iota(jnp.int32, (64, 320), 0)
        in_row = lax.broadcasted_iota(jnp.int32, (64, 320), 1)
        down_by = (in_row >> 5) - 2 * (out_row >> 4)
        along_by = (in_row & 31) - 2 * (out_row & 15)
        choose = []
        for kh in range(3):
            for kw in range(3):
                dr, dc = down_by - (2 - kh), along_by - (1 - kw)
                hit = ((dr == 0) | (dr == 1)) & ((dc == 0) | (dc == 1))
                choose.append(jnp.where(hit, 1.0, 0.0).astype(F32))
        chosen = jnp.concatenate(choose, axis=0).astype(BF)

        def one(f, carry):
            total = jnp.dot(chosen, padded[f].reshape(320, 256), preferred_element_type=F32)
            top = total.astype(BF)
            rest = (total - top.astype(F32)).astype(BF)
            windows[f, 0] = top.reshape(9, 64, 256)
            windows[f, 1] = rest.reshape(9, 64, 256)
            return carry

        lax.fori_loop(0, 5, one, 0)

    def make_slope(total):
        gs = unfold_groups(total) * (1.0 / COUNT)
        mean, msq = gs[0:4], gs[4:8]
        rstd = lax.rsqrt(msq - mean * mean + EPSILON)
        mean_row, rstd_row = row_of(mean, 0), row_of(rstd, 0)
        gain, bias = gain_ref[...], bias_ref[...]

        def one(i, carry):
            value = (y_ref[i // 4, lax.rem(i, 4)].astype(F32) - mean_row) * rstd_row
            pre = value * gain + bias
            sig = jax.nn.sigmoid(pre)
            hat[i] = value
            slope[i] = sig * (1.0 + pre * (1.0 - sig)) * gain
            return carry

        lax.fori_loop(0, 12, one, 0)
        return rstd_row

    pl.semaphore_wait(barrier, len(partners))
    stage_a_send()
    frames_begin()
    ar_begin(0, 0, stats)
    frames_choose()

    @pl.when(c == 0)
    def _():
        stage_a_arrive(0)
        begin(0)

    @pl.when(c == 1)
    def _():
        stage_a_arrive(1)
        begin(1)

    ar_begin(0, 1, ar_end(0, 0))
    frames_pass()

    @pl.when(c == 0)
    def _():
        y_in0(1)
        x_in0(0)

    @pl.when(c == 1)
    def _():
        x_in1()

    rstd_row = make_slope(ar_end(0, 1))

    @pl.when(c == 0)
    def _():
        y_in0(2)
        x_in0(1)
        o_in0(0)
        x_in0(2)

    @pl.when(c == 1)
    def _():
        y_in1(1, (0,))
        o_in1()
        y_in1(1, (1, 2))

    order_frames()

    @pl.when(c == 0)
    def _():
        y_in0(3)
        o_in0(1)
        x_in0(3)
        o_in0(2)
        x_in0(4)
        y_in0(4)

    @pl.when(c == 1)
    def _():
        y_in1(1, (3,))
        y_in1(2)

    finish_rows()
    make_windows()

    @pl.when(c == 0)
    def _():
        o_in0(3)
        x_in0(5)
        o_in0(4)
        x_in0(6)
        o_in0(5)
        x_in0(7)
        o_in0(6)
        for k in range(8):
            tables[1].arrive(*[f"d{k}{j}" for j in range(4)])

    @pl.when(c == 1)
    def _():
        y_in1(3)
        y_in1(4)

    def kernel_rows(first_tap, n):
        block = whole[pl.ds(first_tap, n)]
        return jnp.concatenate([block[:, k].reshape(n * 256, 128) for k in range(4)], axis=1)

    def taps_of(i, carry):
        kt, kh = i // 3, lax.rem(i, 3)
        lhs = jnp.concatenate(
            [windows[pl.ds(2 - kt, 3), :, kh * 3 + kw].reshape(384, 256) for kw in range(3)], axis=1
        )
        acc[...] += jnp.dot(lhs, kernel_rows(3 * i, 3), preferred_element_type=F32).reshape(3, 2, 64, 512)
        return carry

    skip[...] = jnp.dot(
        windows[0:3, :, 4].reshape(384, 256), kernel_rows(27, 1), preferred_element_type=F32
    ).reshape(3, 2, 64, 512)
    acc[...] = jnp.zeros_like(acc)
    lax.fori_loop(TAPS[1][0] // 3, 9, taps_of, 0)

    @pl.when(c == 0)
    def _():
        o_in0(7)

    @pl.when(c == 1)
    def _():
        for k in range(8):
            tables[0].arrive(*[f"d{k}{j}" for j in range(4)])

    lax.fori_loop(0, TAPS[1][0] // 3, taps_of, 0)

    one_sum = jnp.zeros((16, 512), F32)
    two_sum = jnp.zeros((16, 512), F32)
    for f in range(3):
        for r in range(4):
            here = slice(16 * r, 16 * r + 16)
            live = jnp.where((f < fl) & (r < rl), 1.0, 0.0).astype(F32)
            grad = (acc[f, 0, here] + acc[f, 1, here]) * slope[4 * f + r]
            slope[4 * f + r] = grad
            one_sum = one_sum + grad * live
            two_sum = two_sum + grad * hat[4 * f + r] * live
    sums = fold_groups(jnp.sum(one_sum, axis=0, keepdims=True), jnp.sum(two_sum, axis=0, keepdims=True))
    ar_begin(1, 0, sums)
    ar_begin(1, 1, ar_end(1, 0))
    both = unfold_groups(ar_end(1, 1)) * (1.0 / COUNT)
    b_one, b_two = row_of(both, 0), row_of(both, 4)
    for f in range(3):
        for r in range(4):
            here = slice(16 * r, 16 * r + 16)
            live = jnp.where((f < fl) & (r < rl), 1.0, 0.0).astype(F32)
            value = rstd_row * (slope[4 * f + r] - (b_one + hat[4 * f + r] * b_two))
            out_ref[f, r] = (value + (skip[f, 0, here] + skip[f, 1, here])) * live

    stage_a_sent()
    for role, sent_by in ((0, (1, 2)), (1, (0, 3))):
        @pl.when(c == role)
        def _():
            for which in sent_by:
                small_copy(which).wait_send()
    for which in (4, 5):
        small_copy(which).wait_send()
    for turn in range(2):
        for step in range(2):
            for k in range((31, 15)[step]):
                ar_copy(turn, step, k).wait_send()
    for role in (0, 1):
        @pl.when(c == role)
        def _():
            tables[role].sent(*[n for n in tables[role].entries if n[0] != "a"])


def shards(coarse_input, cotangent, conv_kernel, short_kernel, norm_gain, norm_bias, frame_lengths, row_lengths):
    vmem = pl.BlockSpec(memory_space=pltpu.VMEM)
    anywhere = pl.BlockSpec(memory_space=pl.ANY)
    copies = (7 + 48 + 14 + 32, 7 + 6 + 56 + 32)
    return pl.pallas_call(
        kernel,
        out_shape=jax.ShapeDtypeStruct((3, 4, 16, 512), F32),
        in_specs=[anywhere] * 8,
        out_specs=vmem,
        scratch_shapes=[
            pltpu.SMEM((64,), jnp.int32),
            pltpu.SMEM((8,), jnp.int32),
            pltpu.VMEM((3, 4, 16, 512), BF),
            pltpu.VMEM((3, 8, 32, 256), BF),
            pltpu.VMEM((1, 512), F32),
            pltpu.VMEM((1, 512), F32),
            pltpu.SemaphoreType.DMA((8,)),
            pltpu.VMEM((28, 4, 256, 128), BF),
            pltpu.VMEM((28, 4, 512), BF),
            pltpu.VMEM((18, 8, 4, 128), BF),
            pltpu.VMEM((18, 32, 128), F32),
            pltpu.VMEM((3, 8, 32, 256), BF),
            pltpu.VMEM((8, 32, 256), BF),
            pltpu.VMEM((2, 5, 32, 256), BF),
            pltpu.VMEM((2, 5, 32, 256), BF),
            pltpu.VMEM((5, 10, 32, 256), BF),
            pltpu.VMEM((5, 2, 9, 64, 256), BF),
            pltpu.VMEM((3, 2, 64, 512), F32),
            pltpu.VMEM((3, 2, 64, 512), F32),
            pltpu.VMEM((12, 16, 512), F32),
            pltpu.VMEM((12, 16, 512), F32),
            pltpu.VMEM((2, 32, 1, 128), F32),
            pltpu.VMEM((2, 16, 1, 128), F32),
            pltpu.SemaphoreType.DMA((2, 31)),
            pltpu.SemaphoreType.DMA((2, 31)),
            pltpu.SemaphoreType.DMA((2, 15)),
            pltpu.SemaphoreType.DMA((2, 15)),
            pltpu.SemaphoreType.DMA((6,)),
            pltpu.SemaphoreType.DMA((6,)),
            pltpu.SemaphoreType.DMA((copies[0],)),
            pltpu.SemaphoreType.DMA((copies[0],)),
            pltpu.SemaphoreType.DMA((copies[1],)),
            pltpu.SemaphoreType.DMA((copies[1],)),
        ],
        compiler_params=pltpu.CompilerParams(
            collective_id=0, has_side_effects=True, vmem_limit_bytes=60 * 1024 * 1024
        ),
    )(
        frame_lengths, row_lengths, coarse_input, cotangent,
        conv_kernel.transpose(0, 2, 1), short_kernel.transpose(0, 2, 1),
        norm_gain.reshape(1, 512), norm_bias.reshape(1, 512),
    )


def solution(mesh):
    return jax.shard_map(
        shards,
        mesh=mesh,
        in_specs=(
            P("tm", "height", None, None),
            P("tm", "height", None, None),
            P(None, None, "tm"),
            P(None, None, "tm"),
            P(),
            P(),
            P(),
            P(),
        ),
        out_specs=P("tm", "height", None, None),
        check_vma=False,
    )
```

time: 87 us -> 75.7 us (0.87)
  Pallas kernels: 81.7 us -> 73.8 us
  local copies, waits for them, and re-layouts: 4.94 us -> 1.77 us
    pallas_call x1, Pallas kernels: 81.7 us -> 73.8 us  [shards(): pl.pallas_call(kernel, out_shape=jax.ShapeDtypeStruct((3, 4, 16, 512), F3...]
    unnamed x17 -> x1, local copies, waits for them, and re-layouts: 4.94 us -> 1.77 us
where the time goes in v2:
time: 75.7 us; the launch traced here: 75.6 us
  Pallas kernels  73.8 us (97%)
  local copies, waits for them, and re-layouts  1.77 us (2%)
    pallas_call x1, Pallas kernels, shards(): pl.pallas_call(kernel, out_shape=jax.ShapeDtypeStruct((3, 4, 16, 512), F3...  73.8 us
    unnamed x1, local copies, waits for them, and re-layouts  1.77 us

profile of v2, /device:TPU:1, one launch (start us, length us, event | category | flops | bytes accessed | tf_op | source)
XLA Modules:
  0.0 75.6 jit_solution(17431894407633289636)
XLA Ops:
  0.0 73.8 %shard_map.82 = f32[3,4,16,512]{3,2,1,0:T(8,128)} custom-call(s32[64]{0:T(128)} %fl_any.1, s32[8]{0:T(128)} %rl_any.1, bf16[3,4,16,512]{3,2,1,0:T(8,128)(2,1)} %y_any.1, bf16[3,8,32,256]{3,2,1,0:T(8,128)(2,1)} %g_any.1, bf16[27,4,512]{2,1,0:T(4,128)(2,1)} %bitcast.4, bf16[1,4,512]{2,1,0:T(4,128)(2,1)} %bitcast.5, f32[1,512]{1,0:T(1,128)} %bitcast.6, ...), custom_call_target="tpu_custom_call" | custom-call | tf_op jit(solution)/shard_map/pallas_call | solution.py:628
  73.8 1.8 %copy.10 = f32[3,4,16,512]{3,2,1,0:T(8,128)} copy(f32[3,4,16,512]{3,2,1,0:T(8,128)} %shard_map.82) | data formatting | bytes 786432

commit v3 on v2

--- a/solution.py
+++ b/solution.py
@@ -9,7 +9,7 @@
 
 EPSILON = 1e-06
 COUNT = 422144.0
-TAPS = ((0, 18), (18, 10))
+TAPS = ((0, 16), (16, 12))
 BF = jnp.bfloat16
 F32 = jnp.float32
 
@@ -67,7 +67,7 @@
 def kernel(
     fl_any, rl_any, y_any, g_any, wc_any, ws_any, gain_any, bias_any, out_ref,
     fl_ref, rl_ref, y_ref, g_ref, gain_ref, bias_ref, load_sem,
-    whole, mine, slots, rows32, ahead, chosen_next, edge_out, edge_in, padded, windows,
+    whole, mine, slots, rows32, ahead, chosen_next, edge_out, edge_in, padded, chosen, windows,
     acc, skip, hat, slope, plane, column, plane_send, plane_recv, column_send, column_recv,
     small_send, small_recv, send0, recv0, send1, recv1,
 ):
@@ -96,16 +96,12 @@
     loads = [
         pltpu.make_async_copy(src, dst, load_sem.at[k])
         for k, (src, dst) in enumerate((
-            (fl_any, fl_ref), (rl_any, rl_ref), (y_any, y_ref), (wc_any, mine.at[pl.ds(0, 27)]),
-            (ws_any, mine.at[pl.ds(27, 1)]), (g_any, g_ref), (gain_any, gain_ref), (bias_any, bias_ref),
+            (wc_any, mine.at[pl.ds(0, 27)]), (ws_any, mine.at[pl.ds(27, 1)]), (g_any, g_ref), (fl_any, fl_ref),
+            (rl_any, rl_ref), (y_any, y_ref), (gain_any, gain_ref), (bias_any, bias_ref),
         ))
     ]
     for load in loads:
         load.start()
-    loads[0].wait()
-    loads[1].wait()
-    fl, rl = fl_ref[tm], rl_ref[height]
-    fl_next = fl_ref[mod(tm + 1, 64)]
 
     def ar_copy(turn, step, k):
         if step == 0:
@@ -152,19 +148,6 @@
     def unfold_groups(row):
         tile = jnp.where(own_lanes, jnp.broadcast_to(row, (8, 128)), 0.0)
         return jnp.dot(tile, unfold, precision=lax.Precision.HIGHEST, preferred_element_type=F32)
-
-    loads[2].wait()
-    first = jnp.zeros((16, 512), F32)
-    second = jnp.zeros((16, 512), F32)
-    for f in range(3):
-        for r in range(4):
-            live = jnp.where((f < fl) & (r < rl), 1.0, 0.0).astype(F32)
-            value = y_ref[f, r].astype(F32) * live
-            first = first + value
-            second = second + value * value
-    stats = fold_groups(jnp.sum(first, axis=0, keepdims=True), jnp.sum(second, axis=0, keepdims=True))
-    for load in loads[3:]:
-        load.wait()
 
     def table(role):
         t0, taps = TAPS[role]
@@ -432,7 +415,7 @@
                 padded[p, r + 1] = lax.select(r == 2 * rl, below, padded[p, r + 1])
             padded[p, 9] = lax.select(rl == 4, below, zero_row)
 
-    def make_windows():
+    def make_chosen():
         out_row = lax.broadcasted_iota(jnp.int32, (64, 320), 0)
         in_row = lax.broadcasted_iota(jnp.int32, (64, 320), 1)
         down_by = (in_row >> 5) - 2 * (out_row >> 4)
@@ -443,17 +426,15 @@
                 dr, dc = down_by - (2 - kh), along_by - (1 - kw)
                 hit = ((dr == 0) | (dr == 1)) & ((dc == 0) | (dc == 1))
                 choose.append(jnp.where(hit, 1.0, 0.0).astype(F32))
-        chosen = jnp.concatenate(choose, axis=0).astype(BF)
-
-        def one(f, carry):
-            total = jnp.dot(chosen, padded[f].reshape(320, 256), preferred_element_type=F32)
+        chosen[...] = jnp.concatenate(choose, axis=0).astype(BF)
+
+    def make_windows(*frames):
+        for f in frames:
+            total = jnp.dot(chosen[...], padded[f].reshape(320, 256), preferred_element_type=F32)
             top = total.astype(BF)
             rest = (total - top.astype(F32)).astype(BF)
             windows[f, 0] = top.reshape(9, 64, 256)
             windows[f, 1] = rest.reshape(9, 64, 256)
-            return carry
-
-        lax.fori_loop(0, 5, one, 0)
 
     def make_slope(total):
         gs = unfold_groups(total) * (1.0 / COUNT)
@@ -473,11 +454,26 @@
         lax.fori_loop(0, 12, one, 0)
         return rstd_row
 
+    loads[0].wait()
+    loads[1].wait()
     pl.semaphore_wait(barrier, len(partners))
     stage_a_send()
-    frames_begin()
+    for load in loads[2:]:
+        load.wait()
+    fl, rl = fl_ref[tm], rl_ref[height]
+    fl_next = fl_ref[mod(tm + 1, 64)]
+
+    first = jnp.zeros((16, 512), F32)
+    second = jnp.zeros((16, 512), F32)
+    for f in range(3):
+        for r in range(4):
+            live = jnp.where((f < fl) & (r < rl), 1.0, 0.0).astype(F32)
+            value = y_ref[f, r].astype(F32) * live
+            first = first + value
+            second = second + value * value
+    stats = fold_groups(jnp.sum(first, axis=0, keepdims=True), jnp.sum(second, axis=0, keepdims=True))
     ar_begin(0, 0, stats)
-    frames_choose()
+    make_chosen()
 
     @pl.when(c == 0)
     def _():
@@ -489,8 +485,9 @@
         stage_a_arrive(1)
         begin(1)
 
+    frames_begin()
     ar_begin(0, 1, ar_end(0, 0))
-    frames_pass()
+    frames_choose()
 
     @pl.when(c == 0)
     def _():
@@ -501,6 +498,7 @@
     def _():
         x_in1()
 
+    frames_pass()
     rstd_row = make_slope(ar_end(0, 1))
 
     @pl.when(c == 0)
@@ -516,41 +514,73 @@
         o_in1()
         y_in1(1, (1, 2))
 
-    order_frames()
-
     @pl.when(c == 0)
     def _():
         y_in0(3)
         o_in0(1)
         x_in0(3)
+
+    @pl.when(c == 1)
+    def _():
+        y_in1(1, (3,))
+        y_in1(2, (0, 1))
+
+    order_frames()
+
+    @pl.when(c == 0)
+    def _():
         o_in0(2)
         x_in0(4)
         y_in0(4)
 
     @pl.when(c == 1)
     def _():
-        y_in1(1, (3,))
-        y_in1(2)
+        y_in1(2, (2, 3))
 
     finish_rows()
-    make_windows()
 
     @pl.when(c == 0)
     def _():
         o_in0(3)
         x_in0(5)
+
+    @pl.when(c == 1)
+    def _():
+        y_in1(3, (0, 1))
+
+    make_windows(0, 1)
+
+    @pl.when(c == 0)
+    def _():
         o_in0(4)
         x_in0(6)
+
+    @pl.when(c == 1)
+    def _():
+        y_in1(3, (2, 3))
+
+    make_windows(2, 3)
+
+    @pl.when(c == 0)
+    def _():
         o_in0(5)
         x_in0(7)
+
+    @pl.when(c == 1)
+    def _():
+        y_in1(4, (0, 1))
+
+    make_windows(4)
+
+    @pl.when(c == 0)
+    def _():
         o_in0(6)
         for k in range(8):
             tables[1].arrive(*[f"d{k}{j}" for j in range(4)])
 
     @pl.when(c == 1)
     def _():
-        y_in1(3)
-        y_in1(4)
+        y_in1(4, (2, 3))
 
     def kernel_rows(first_tap, n):
         block = whole[pl.ds(first_tap, n)]
@@ -568,7 +598,7 @@
         windows[0:3, :, 4].reshape(384, 256), kernel_rows(27, 1), preferred_element_type=F32
     ).reshape(3, 2, 64, 512)
     acc[...] = jnp.zeros_like(acc)
-    lax.fori_loop(TAPS[1][0] // 3, 9, taps_of, 0)
+    lax.fori_loop(6, 9, taps_of, 0)
 
     @pl.when(c == 0)
     def _():
@@ -579,7 +609,7 @@
         for k in range(8):
             tables[0].arrive(*[f"d{k}{j}" for j in range(4)])
 
-    lax.fori_loop(0, TAPS[1][0] // 3, taps_of, 0)
+    lax.fori_loop(0, 6, taps_of, 0)
 
     one_sum = jnp.zeros((16, 512), F32)
     two_sum = jnp.zeros((16, 512), F32)
@@ -593,7 +623,21 @@
             two_sum = two_sum + grad * hat[4 * f + r] * live
     sums = fold_groups(jnp.sum(one_sum, axis=0, keepdims=True), jnp.sum(two_sum, axis=0, keepdims=True))
     ar_begin(1, 0, sums)
+    stage_a_sent()
+    for role, sent_by in ((0, (1, 2)), (1, (0, 3))):
+        @pl.when(c == role)
+        def _():
+            for which in sent_by:
+                small_copy(which).wait_send()
+            tables[role].sent(*[n for n in tables[role].entries if n[0] != "a"])
+    for which in (4, 5):
+        small_copy(which).wait_send()
+    for step in range(2):
+        for k in range((31, 15)[step]):
+            ar_copy(0, step, k).wait_send()
     ar_begin(1, 1, ar_end(1, 0))
+    for k in range(31):
+        ar_copy(1, 0, k).wait_send()
     both = unfold_groups(ar_end(1, 1)) * (1.0 / COUNT)
     b_one, b_two = row_of(both, 0), row_of(both, 4)
     for f in range(3):
@@ -602,23 +646,8 @@
             live = jnp.where((f < fl) & (r < rl), 1.0, 0.0).astype(F32)
             value = rstd_row * (slope[4 * f + r] - (b_one + hat[4 * f + r] * b_two))
             out_ref[f, r] = (value + (skip[f, 0, here] + skip[f, 1, here])) * live
-
-    stage_a_sent()
-    for role, sent_by in ((0, (1, 2)), (1, (0, 3))):
-        @pl.when(c == role)
-        def _():
-            for which in sent_by:
-                small_copy(which).wait_send()
-    for which in (4, 5):
-        small_copy(which).wait_send()
-    for turn in range(2):
-        for step in range(2):
-            for k in range((31, 15)[step]):
-                ar_copy(turn, step, k).wait_send()
-    for role in (0, 1):
-        @pl.when(c == role)
-        def _():
-            tables[role].sent(*[n for n in tables[role].entries if n[0] != "a"])
+    for k in range(15):
+        ar_copy(1, 1, k).wait_send()
 
 
 def shards(coarse_input, cotangent, conv_kernel, short_kernel, norm_gain, norm_bias, frame_lengths, row_lengths):
@@ -640,13 +669,14 @@
             pltpu.SemaphoreType.DMA((8,)),
             pltpu.VMEM((28, 4, 256, 128), BF),
             pltpu.VMEM((28, 4, 512), BF),
-            pltpu.VMEM((18, 8, 4, 128), BF),
-            pltpu.VMEM((18, 32, 128), F32),
+            pltpu.VMEM((17, 8, 4, 128), BF),
+            pltpu.VMEM((17, 32, 128), F32),
             pltpu.VMEM((3, 8, 32, 256), BF),
             pltpu.VMEM((8, 32, 256), BF),
             pltpu.VMEM((2, 5, 32, 256), BF),
             pltpu.VMEM((2, 5, 32, 256), BF),
             pltpu.VMEM((5, 10, 32, 256), BF),
+            pltpu.VMEM((576, 320), BF),
             pltpu.VMEM((5, 2, 9, 64, 256), BF),
             pltpu.VMEM((3, 2, 64, 512), F32),
             pltpu.VMEM((3, 2, 64, 512), F32),

time: 75.7 us -> 71.4 us (0.943)
  Pallas kernels: 73.8 us -> 69.5 us
    pallas_call x1, Pallas kernels: 73.8 us -> 69.5 us  [shards(): pl.pallas_call(kernel, out_shape=jax.ShapeDtypeStruct((3, 4, 16, 512), F3...]
where the time goes in v3:
time: 71.4 us; the launch traced here: 71.3 us
  Pallas kernels  69.5 us (97%)
  local copies, waits for them, and re-layouts  1.77 us (2%)
    pallas_call x1, Pallas kernels, shards(): pl.pallas_call(kernel, out_shape=jax.ShapeDtypeStruct((3, 4, 16, 512), F3...  69.5 us
    unnamed x1, local copies, waits for them, and re-layouts  1.77 us

profile of v3, /device:TPU:1, one launch (start us, length us, event | category | flops | bytes accessed | tf_op | source)
XLA Modules:
  0.0 71.3 jit_solution(13560226336768782492)
XLA Ops:
  0.0 69.5 %shard_map.82 = f32[3,4,16,512]{3,2,1,0:T(8,128)} custom-call(s32[64]{0:T(128)} %fl_any.1, s32[8]{0:T(128)} %rl_any.1, bf16[3,4,16,512]{3,2,1,0:T(8,128)(2,1)} %y_any.1, bf16[3,8,32,256]{3,2,1,0:T(8,128)(2,1)} %g_any.1, bf16[27,4,512]{2,1,0:T(4,128)(2,1)} %bitcast.4, bf16[1,4,512]{2,1,0:T(4,128)(2,1)} %bitcast.5, f32[1,512]{1,0:T(1,128)} %bitcast.6, ...), custom_call_target="tpu_custom_call" | custom-call | tf_op jit(solution)/shard_map/pallas_call | solution.py:657
  69.5 1.8 %copy.10 = f32[3,4,16,512]{3,2,1,0:T(8,128)} copy(f32[3,4,16,512]{3,2,1,0:T(8,128)} %shard_map.82) | data formatting | bytes 786432

commit v4 on v3

--- a/solution.py
+++ b/solution.py
@@ -10,6 +10,7 @@
 EPSILON = 1e-06
 COUNT = 422144.0
 TAPS = ((0, 16), (16, 12))
+SHARED = 6
 BF = jnp.bfloat16
 F32 = jnp.float32
 
@@ -93,10 +94,12 @@
     barrier = pltpu.get_barrier_semaphore()
     for partner in partners:
         pl.semaphore_signal(barrier, inc=1, device_id=partner, device_id_type=pl.DeviceIdType.MESH)
+    lanes = pl.ds(pl.multiple_of(x * 128, 128), 128)
     loads = [
         pltpu.make_async_copy(src, dst, load_sem.at[k])
         for k, (src, dst) in enumerate((
-            (wc_any, mine.at[pl.ds(0, 27)]), (ws_any, mine.at[pl.ds(27, 1)]), (g_any, g_ref), (fl_any, fl_ref),
+            (wc_any.at[:, :, lanes], mine.at[pl.ds(0, 27)]), (ws_any.at[:, :, lanes], mine.at[pl.ds(27, 1)]),
+            (g_any, g_ref), (fl_any, fl_ref),
             (rl_any, rl_ref), (y_any, y_ref), (gain_any, gain_ref), (bias_any, bias_ref),
         ))
     ]
@@ -158,9 +161,8 @@
             row = pl.multiple_of(block * 32, 32)
             return whole.at[pl.ds(t0 + lo, n), column, pl.ds(row, 32)]
 
-        lane = pl.multiple_of(x * 128, 128)
-        src = mine.at[pl.ds(t0, taps), :, pl.ds(lane, 128)]
-        place = slots.at[pl.ds(0, taps), h * 2 + c]
+        src = mine.at[pl.ds(t0, taps)]
+        place = slots.at[h * 2 + c, pl.ds(0, taps)]
         for d in range(1, 4):
             device = at(z_=mod(z + (2 * zl - 1) * d, 8), c_=role)
             t.add(f"a{d}0", src, place, device)
@@ -183,6 +185,9 @@
             t.add(f"or{k}", ref, ref, right)
             ref = piece(columns[2], blocks[k], *parts[1])
             t.add(f"ol{k}", ref, ref, left)
+            if role == 0 and k < SHARED:
+                ref = piece(columns[3], blocks[k])
+                t.add(f"zo{k}", ref, ref, at(z_=z + 1 - 2 * zl))
         for j in range(1 if role == 0 else 4):
             for s in range(4):
                 for q in (0, 1):
@@ -235,14 +240,13 @@
     def stage_a_arrive(role):
         t0, taps = TAPS[role]
         t = tables[role]
-        lane = pl.multiple_of(x * 128, 128)
-        slots[0:taps, h * 2 + role] = mine[t0 : t0 + taps, :, pl.ds(lane, 128)]
+        slots[h * 2 + role, 0:taps] = mine[t0 : t0 + taps]
         for d in range(1, 4):
             t.arrive(f"a{d}0", f"a{d}1")
         t.arrive("as")
         row = pl.multiple_of(y * 32, 32)
         for s in range(8):
-            rows32[0:taps, 4 * s : 4 * s + 4] = slots[0:taps, s].astype(F32)
+            rows32[0:taps, 4 * s : 4 * s + 4] = slots[s, 0:taps].astype(F32)
         whole[t0 : t0 + taps, x, pl.ds(row, 32)] = rows32[0:taps].astype(BF)
 
     def begin(role):
@@ -252,12 +256,20 @@
             t.start(*(both if role == 0 else both[2:] + both[:2]))
         t.start("d00")
 
+    def mine_to_fetch(k, act, otherwise=None):
+        if k >= SHARED:
+            act()
+            return
+        pl.when(zl == k % 2)(act)
+        if otherwise is not None:
+            pl.when(zl != k % 2)(otherwise)
+
     def x_in0(k):
         t = tables[0]
         t.arrive(f"xr{k}0")
-        t.start(f"or{k}")
+        mine_to_fetch(k, lambda: t.start(f"or{k}"))
         t.arrive(f"xl{k}1")
-        t.start(f"ol{k}")
+        mine_to_fetch(k, lambda: t.start(f"ol{k}"))
         t.arrive(f"xr{k}1")
         t.start(f"d{k}1")
         t.arrive(f"xl{k}0")
@@ -265,8 +277,20 @@
 
     def o_in0(k):
         t = tables[0]
-        t.arrive(f"or{k}", f"ol{k}")
-        t.start(f"d{k}3")
+
+        def fetched():
+            t.arrive(f"or{k}", f"ol{k}")
+            if k < SHARED:
+                t.start(f"zo{k}")
+            t.start(f"d{k}3")
+
+        def given():
+            t.arrive(f"zo{k - 2}")
+            t.start(f"d{k - 2}3")
+
+        mine_to_fetch(k, fetched)
+        if 0 <= k - 2 < SHARED:
+            pl.when(zl != k % 2)(given)
 
     def y_in0(s):
         t = tables[0]
@@ -436,11 +460,14 @@
             windows[f, 0] = top.reshape(9, 64, 256)
             windows[f, 1] = rest.reshape(9, 64, 256)
 
-    def make_slope(total):
+    def statistics(total):
         gs = unfold_groups(total) * (1.0 / COUNT)
         mean, msq = gs[0:4], gs[4:8]
         rstd = lax.rsqrt(msq - mean * mean + EPSILON)
         mean_row, rstd_row = row_of(mean, 0), row_of(rstd, 0)
+        return mean_row, rstd_row
+
+    def make_slope(low, high, mean_row, rstd_row):
         gain, bias = gain_ref[...], bias_ref[...]
 
         def one(i, carry):
@@ -451,8 +478,7 @@
             slope[i] = sig * (1.0 + pre * (1.0 - sig)) * gain
             return carry
 
-        lax.fori_loop(0, 12, one, 0)
-        return rstd_row
+        lax.fori_loop(low, high, one, 0)
 
     loads[0].wait()
     loads[1].wait()
@@ -497,9 +523,10 @@
     @pl.when(c == 1)
     def _():
         x_in1()
+        y_in1(1, (0,))
+        o_in1()
 
     frames_pass()
-    rstd_row = make_slope(ar_end(0, 1))
 
     @pl.when(c == 0)
     def _():
@@ -510,9 +537,7 @@
 
     @pl.when(c == 1)
     def _():
-        y_in1(1, (0,))
-        o_in1()
-        y_in1(1, (1, 2))
+        y_in1(1, (1, 2, 3))
 
     @pl.when(c == 0)
     def _():
@@ -522,7 +547,6 @@
 
     @pl.when(c == 1)
     def _():
-        y_in1(1, (3,))
         y_in1(2, (0, 1))
 
     order_frames()
@@ -537,7 +561,8 @@
     def _():
         y_in1(2, (2, 3))
 
-    finish_rows()
+    mean_row, rstd_row = statistics(ar_end(0, 1))
+    make_slope(0, 6, mean_row, rstd_row)
 
     @pl.when(c == 0)
     def _():
@@ -548,6 +573,7 @@
     def _():
         y_in1(3, (0, 1))
 
+    finish_rows()
     make_windows(0, 1)
 
     @pl.when(c == 0)
@@ -571,6 +597,7 @@
         y_in1(4, (0, 1))
 
     make_windows(4)
+    make_slope(6, 12, mean_row, rstd_row)
 
     @pl.when(c == 0)
     def _():
@@ -629,7 +656,11 @@
         def _():
             for which in sent_by:
                 small_copy(which).wait_send()
-            tables[role].sent(*[n for n in tables[role].entries if n[0] != "a"])
+            shared = [n + str(k) for k in range(SHARED) for n in ("or", "ol", "zo")] if role == 0 else []
+            tables[role].sent(*[n for n in tables[role].entries if n[0] != "a" and n not in shared])
+            if role == 0:
+                for k in range(SHARED):
+                    mine_to_fetch(k, lambda k=k: tables[0].sent(f"or{k}", f"ol{k}", f"zo{k}"))
     for which in (4, 5):
         small_copy(which).wait_send()
     for step in range(2):
@@ -653,7 +684,7 @@
 def shards(coarse_input, cotangent, conv_kernel, short_kernel, norm_gain, norm_bias, frame_lengths, row_lengths):
     vmem = pl.BlockSpec(memory_space=pltpu.VMEM)
     anywhere = pl.BlockSpec(memory_space=pl.ANY)
-    copies = (7 + 48 + 14 + 32, 7 + 6 + 56 + 32)
+    copies = (7 + 48 + SHARED + 14 + 32, 7 + 6 + 56 + 32)
     return pl.pallas_call(
         kernel,
         out_shape=jax.ShapeDtypeStruct((3, 4, 16, 512), F32),
@@ -668,8 +699,8 @@
             pltpu.VMEM((1, 512), F32),
             pltpu.SemaphoreType.DMA((8,)),
             pltpu.VMEM((28, 4, 256, 128), BF),
-            pltpu.VMEM((28, 4, 512), BF),
-            pltpu.VMEM((17, 8, 4, 128), BF),
+            pltpu.VMEM((28, 4, 128), BF),
+            pltpu.VMEM((8, 17, 4, 128), BF),
             pltpu.VMEM((17, 32, 128), F32),
             pltpu.VMEM((3, 8, 32, 256), BF),
             pltpu.VMEM((8, 32, 256), BF),

time: 71.4 us -> 71 us (level)
  no operation moved by 1% of the time
where the time goes in v4:
time: 71 us; the launch traced here: 70.8 us
  Pallas kernels  69.1 us (97%)
  local copies, waits for them, and re-layouts  1.77 us (2%)
    pallas_call x1, Pallas kernels, shards(): pl.pallas_call(kernel, out_shape=jax.ShapeDtypeStruct((3, 4, 16, 512), F3...  69.1 us
    unnamed x1, local copies, waits for them, and re-layouts  1.77 us

profile of v4, /device:TPU:1, one launch (start us, length us, event | category | flops | bytes accessed | tf_op | source)
XLA Modules:
  0.0 70.8 jit_solution(11613072596341326030)
XLA Ops:
  0.0 69.1 %shard_map.82 = f32[3,4,16,512]{3,2,1,0:T(8,128)} custom-call(s32[64]{0:T(128)} %fl_any.1, s32[8]{0:T(128)} %rl_any.1, bf16[3,4,16,512]{3,2,1,0:T(8,128)(2,1)} %y_any.1, bf16[3,8,32,256]{3,2,1,0:T(8,128)(2,1)} %g_any.1, bf16[27,4,512]{2,1,0:T(4,128)(2,1)} %bitcast.4, bf16[1,4,512]{2,1,0:T(4,128)(2,1)} %bitcast.5, f32[1,512]{1,0:T(1,128)} %bitcast.6, ...), custom_call_target="tpu_custom_call" | custom-call | tf_op jit(solution)/shard_map/pallas_call | solution.py:688
  69.1 1.8 %copy.10 = f32[3,4,16,512]{3,2,1,0:T(8,128)} copy(f32[3,4,16,512]{3,2,1,0:T(8,128)} %shard_map.82) | data formatting | bytes 786432

commit v5 on v4

--- a/solution.py
+++ b/solution.py
@@ -9,7 +9,7 @@
 
 EPSILON = 1e-06
 COUNT = 422144.0
-TAPS = ((0, 16), (16, 12))
+TAPS = ((0, 15), (15, 13))
 SHARED = 6
 BF = jnp.bfloat16
 F32 = jnp.float32

time: 71 us -> 70.5 us (level)
  no operation moved by 1% of the time
where the time goes in v5:
time: 70.5 us; the launch traced here: 70.3 us
  Pallas kernels  68.5 us (97%)
  local copies, waits for them, and re-layouts  1.77 us (3%)
    pallas_call x1, Pallas kernels, shards(): pl.pallas_call(kernel, out_shape=jax.ShapeDtypeStruct((3, 4, 16, 512), F3...  68.5 us
    unnamed x1, local copies, waits for them, and re-layouts  1.77 us

profile of v5, /device:TPU:1, one launch (start us, length us, event | category | flops | bytes accessed | tf_op | source)
XLA Modules:
  0.0 70.3 jit_solution(419599190411932332)
XLA Ops:
  0.0 68.5 %shard_map.82 = f32[3,4,16,512]{3,2,1,0:T(8,128)} custom-call(s32[64]{0:T(128)} %fl_any.1, s32[8]{0:T(128)} %rl_any.1, bf16[3,4,16,512]{3,2,1,0:T(8,128)(2,1)} %y_any.1, bf16[3,8,32,256]{3,2,1,0:T(8,128)(2,1)} %g_any.1, bf16[27,4,512]{2,1,0:T(4,128)(2,1)} %bitcast.4, bf16[1,4,512]{2,1,0:T(4,128)(2,1)} %bitcast.5, f32[1,512]{1,0:T(1,128)} %bitcast.6, ...), custom_call_target="tpu_custom_call" | custom-call | tf_op jit(solution)/shard_map/pallas_call | solution.py:688
  68.5 1.8 %copy.10 = f32[3,4,16,512]{3,2,1,0:T(8,128)} copy(f32[3,4,16,512]{3,2,1,0:T(8,128)} %shard_map.82) | data formatting | bytes 786432
